TPU v7x, 32 devices: a whole 2x2x4 slice. The times are simulated.
32 devices in a mesh: dp: 8 (over z, x), blk: 4 (over y, core).
Axes of the slice: x: 2, y: 2, z: 4, core: 2. Of those that a mesh axis runs over, the one named last changes fastest.
Arguments:
- tokens: bfloat16 [8, 1024, 1152], P('dp', 'blk'), may hold values from -6 to 6
- condition: bfloat16 [8, 7, 1152], P('dp'), may hold values from -6 to 6
- segment_ids: int32 [8, 1024], P('dp'), may hold values from 0 to 6, as said below
- qkv_weight: bfloat16 [1152, 3456], P('dp'), may hold values from -0.1875 to 0.1875
- query_bias: bfloat16 [1152], replicated, may hold values from -1.75 to 1.75
- value_bias: bfloat16 [1152], replicated, may hold values from -1.75 to 1.75
- output_weight: bfloat16 [1152, 1152], P('dp'), may hold values from -1.75 to 1.75
- output_bias: bfloat16 [1152], replicated, may hold values from -1.75 to 1.75
- up_weight: bfloat16 [1152, 4608], P('dp'), may hold values from -0.1875 to 0.1875
- up_bias: bfloat16 [4608], replicated, may hold values from -1.75 to 1.75
- down_weight: bfloat16 [4608, 1152], P('dp'), may hold values from -0.1875 to 0.1875
- down_bias: bfloat16 [1152], replicated, may hold values from -1.75 to 1.75
- adaln_weight: bfloat16 [1152, 6912], P('dp'), may hold values from -0.1875 to 0.1875
- adaln_bias: bfloat16 [6912], replicated, may hold values from -1.75 to 1.75
- cotangent: bfloat16 [8, 1024, 1152], P('dp', 'blk'), may hold values from -6 to 6
Outputs:
- output: bfloat16 [8, 1024, 1152], P('dp', 'blk')
- grad_tokens: bfloat16 [8, 1024, 1152], P('dp', 'blk')
- grad_condition: float32 [8, 7, 1152], P('dp')
- grad_qkv_weight: float32 [1152, 3456], P('dp')
- grad_query_bias: float32 [1152], replicated
- grad_value_bias: float32 [1152], replicated
- grad_output_weight: float32 [1152, 1152], P('dp')
- grad_output_bias: float32 [1152], replicated
- grad_up_weight: float32 [1152, 4608], P('dp')
- grad_up_bias: float32 [4608], replicated
- grad_down_weight: float32 [4608, 1152], P('dp')
- grad_down_bias: float32 [1152], replicated
- grad_adaln_weight: float32 [1152, 6912], P('dp')
- grad_adaln_bias: float32 [6912], replicated
Inputs may be any that keep to these rules, and one draw needn't show every extreme that they name: `segment_ids`: Non-decreasing along each sequence, every crop 0 to 6 present; in every sequence one crop begins within the first 256 tokens and ends within the last 256.
All inputs are finite; a program needn't handle non-finite values.
Results may differ from a plain program's by a relative error of at most 0.018.
Values may be sent and summed in bfloat16 or wider, within the bound.
A program may use at most 320 MiB of HBM per device.

v0:
```python
import jax
import jax.numpy as jnp
from jax import lax
from jax.sharding import PartitionSpec as P

HEADS = 16


def shifted(x, axis, by):
    size = lax.axis_size(axis)
    return lax.ppermute(x, axis, [(i, (i + by) % size) for i in range(size)])


def shortened(x):
    return jax.tree.map(lambda a: a.astype(jnp.bfloat16) if a.dtype == jnp.float32 else a, x)


def modulate(rows, shift, scale):
    centre = rows - jnp.mean(rows, axis=-1, keepdims=True)
    normed = centre * lax.rsqrt(jnp.mean(centre * centre, axis=-1, keepdims=True) + 1e-06)
    return normed * (1.0 + scale) + shift


def gelu_tanh(values):
    return jax.nn.gelu(values, approximate=True)


def to_heads(rows):
    return rows.reshape(rows.shape[0], rows.shape[1], HEADS, rows.shape[2] // HEADS)


def column_sums(values):
    return jnp.sum(values.astype(jnp.float32), axis=(0, 1))


def per_device(
    tokens,
    condition,
    segment_ids,
    qkv_weight,
    query_bias,
    value_bias,
    output_weight,
    output_bias,
    up_weight,
    up_bias,
    down_weight,
    down_bias,
    adaln_weight,
    adaln_bias,
    cotangent,
):
    seqs, strip, width = tokens.shape
    blocks = lax.axis_size("blk")
    place = lax.axis_index("blk")
    head_dim = width // HEADS
    factor = head_dim ** (-0.5)
    full_qkv, full_output, full_up, full_down, full_adaln = (
        lax.all_gather(qkv_weight, "dp", axis=0, tiled=True),
        lax.all_gather(output_weight, "dp", axis=0, tiled=True),
        lax.all_gather(up_weight, "dp", axis=0, tiled=True),
        lax.all_gather(down_weight, "dp", axis=0, tiled=True),
        lax.all_gather(adaln_weight, "dp", axis=0, tiled=True),
    )
    crops = condition.shape[1]
    cond_rows = condition.astype(jnp.float32)
    cond_act, silu_back = jax.vjp(jax.nn.silu, cond_rows)
    cond_low = cond_act.astype(jnp.bfloat16)
    modulation = jnp.einsum(
        "scd,de->sce", cond_low, full_adaln, preferred_element_type=jnp.float32
    ) + adaln_bias.astype(jnp.float32)
    own_labels = lax.dynamic_slice_in_dim(segment_ids, place * strip, strip, 1)
    chooser = (own_labels[:, :, None] == jnp.arange(crops, dtype=jnp.int32)[None, None, :]).astype(
        jnp.float32
    )
    per_token = jnp.einsum("stc,sce->ste", chooser, modulation, precision=lax.Precision.HIGHEST)
    shift_a, scale_a, gate_a, shift_m, scale_m, gate_m = jnp.split(per_token, 6, axis=-1)
    rows_in = tokens.astype(jnp.float32)
    normed_a, norm_back_a = jax.vjp(modulate, rows_in, shift_a, scale_a)
    normed_a = normed_a.astype(jnp.bfloat16)
    packed_bias = jnp.concatenate(
        [
            query_bias.astype(jnp.float32),
            jnp.zeros((width,), jnp.float32),
            value_bias.astype(jnp.float32),
        ]
    )
    packed = (jnp.dot(normed_a, full_qkv, preferred_element_type=jnp.float32) + packed_bias).astype(
        jnp.bfloat16
    )
    queries, key_rows, value_rows = jnp.split(packed, 3, axis=-1)
    query_heads = to_heads(queries)
    run_top = jnp.full((seqs, HEADS, strip), -1e30, jnp.float32)
    run_total = jnp.zeros((seqs, HEADS, strip), jnp.float32)
    gathered = jnp.zeros((seqs, HEADS, strip, head_dim), jnp.float32)
    moving_keys, moving_values = (key_rows, value_rows)
    for rounds in range(blocks):
        anchor = (place - rounds) % blocks
        far_labels = lax.dynamic_slice_in_dim(segment_ids, anchor * strip, strip, 1)
        allowed = own_labels[:, None, :, None] == far_labels[:, None, None, :]
        scores = (
            jnp.einsum(
                "sqhd,skhd->shqk",
                query_heads,
                to_heads(moving_keys),
                preferred_element_type=jnp.float32,
            )
            * factor
        )
        scores = jnp.where(allowed, scores, -1e30)
        new_top = jnp.maximum(run_top, jnp.max(scores, axis=-1))
        rescale = jnp.exp(run_top - new_top)
        raised = jnp.where(allowed, jnp.exp(scores - new_top[..., None]), 0.0)
        run_total = run_total * rescale + jnp.sum(raised, axis=-1)
        gathered = gathered * rescale[..., None] + jnp.einsum(
            "shqk,skhd->shqd",
            raised.astype(jnp.bfloat16),
            to_heads(moving_values),
            preferred_element_type=jnp.float32,
        )
        run_top = new_top
        if rounds + 1 < blocks:
            moving_keys, moving_values = shifted((moving_keys, moving_values), "blk", 1)
    attended = gathered / run_total[..., None]
    log_total = run_top + jnp.log(run_total)
    attended_rows = attended.transpose(0, 2, 1, 3).reshape(seqs, strip, width)
    attended_low = attended_rows.astype(jnp.bfloat16)
    branch_a = jnp.dot(
        attended_low, full_output, preferred_element_type=jnp.float32
    ) + output_bias.astype(jnp.float32)
    middle = rows_in + gate_a * branch_a
    normed_m, norm_back_m = jax.vjp(modulate, middle, shift_m, scale_m)
    normed_m = normed_m.astype(jnp.bfloat16)
    hidden = jnp.dot(normed_m, full_up, preferred_element_type=jnp.float32) + up_bias.astype(
        jnp.float32
    )
    active, gelu_back = jax.vjp(gelu_tanh, hidden)
    active = active.astype(jnp.bfloat16)
    branch_m = jnp.dot(active, full_down, preferred_element_type=jnp.float32) + down_bias.astype(
        jnp.float32
    )
    output = (middle + gate_m * branch_m).astype(jnp.bfloat16)
    upstream = cotangent.astype(jnp.float32)
    d_gate_m = upstream * branch_m
    d_branch_m = (gate_m * upstream).astype(jnp.bfloat16)
    grad_down = jnp.einsum("stf,std->fd", active, d_branch_m, preferred_element_type=jnp.float32)
    grad_down_bias = column_sums(d_branch_m)
    d_active = jnp.einsum("std,fd->stf", d_branch_m, full_down, preferred_element_type=jnp.float32)
    d_hidden = gelu_back(d_active)[0].astype(jnp.bfloat16)
    grad_up = jnp.einsum("std,stf->df", normed_m, d_hidden, preferred_element_type=jnp.float32)
    grad_up_bias = column_sums(d_hidden)
    d_normed_m = jnp.einsum("stf,df->std", d_hidden, full_up, preferred_element_type=jnp.float32)
    d_middle_n, d_shift_m, d_scale_m = norm_back_m(d_normed_m)
    d_middle = upstream + d_middle_n
    d_gate_a = d_middle * branch_a
    d_branch_a = (gate_a * d_middle).astype(jnp.bfloat16)
    grad_output = jnp.einsum(
        "std,ste->de", attended_low, d_branch_a, preferred_element_type=jnp.float32
    )
    grad_output_bias = column_sums(d_branch_a)
    d_attended = jnp.einsum(
        "ste,de->std", d_branch_a, full_output, preferred_element_type=jnp.float32
    ).astype(jnp.bfloat16)
    d_heads = to_heads(d_attended)
    delta = jnp.einsum("sqhd,shqd->shq", d_heads.astype(jnp.float32), attended)
    grad_query = jnp.zeros((seqs, strip, HEADS, head_dim), jnp.float32)
    key_sums = jnp.zeros((seqs, strip, width), jnp.float32)
    value_sums = jnp.zeros((seqs, strip, width), jnp.float32)
    cycle_keys, cycle_values = (key_rows, value_rows)
    for rounds in range(blocks):
        anchor = (place - rounds) % blocks
        far_labels = lax.dynamic_slice_in_dim(segment_ids, anchor * strip, strip, 1)
        block_allowed = own_labels[:, None, :, None] == far_labels[:, None, None, :]
        key_heads = to_heads(cycle_keys)
        value_heads = to_heads(cycle_values)
        block_scores = (
            jnp.einsum(
                "sqhd,skhd->shqk", query_heads, key_heads, preferred_element_type=jnp.float32
            )
            * factor
        )
        soft_weights = jnp.where(block_allowed, jnp.exp(block_scores - log_total[..., None]), 0.0)
        d_values = jnp.einsum(
            "shqk,sqhd->skhd",
            soft_weights.astype(jnp.bfloat16),
            d_heads,
            preferred_element_type=jnp.float32,
        )
        d_weights = jnp.einsum(
            "sqhd,skhd->shqk", d_heads, value_heads, preferred_element_type=jnp.float32
        )
        d_scores = (soft_weights * (d_weights - delta[..., None])).astype(jnp.bfloat16)
        d_query = (
            jnp.einsum("shqk,skhd->sqhd", d_scores, key_heads, preferred_element_type=jnp.float32)
            * factor
        )
        d_keys = (
            jnp.einsum("shqk,sqhd->skhd", d_scores, query_heads, preferred_element_type=jnp.float32)
            * factor
        )
        d_query, d_keys, d_values = (
            d_query,
            d_keys.reshape(seqs, -1, width),
            d_values.reshape(seqs, -1, width),
        )
        grad_query = grad_query + d_query
        key_sums, value_sums = (
            shifted(shortened(key_sums + d_keys), "blk", 1),
            shifted((value_sums + d_values).astype(jnp.bfloat16), "blk", 1).astype(jnp.float32),
        )
        if rounds + 1 < blocks:
            cycle_keys, cycle_values = shifted((cycle_keys, cycle_values), "blk", 1)
    d_packed = jnp.concatenate(
        [grad_query.reshape(seqs, strip, width), key_sums, value_sums], axis=-1
    ).astype(jnp.bfloat16)
    grad_qkv = jnp.einsum("std,ste->de", normed_a, d_packed, preferred_element_type=jnp.float32)
    grad_query_bias = column_sums(d_packed[..., :width])
    grad_value_bias = column_sums(d_packed[..., 2 * width :])
    d_normed_a = jnp.einsum("ste,de->std", d_packed, full_qkv, preferred_element_type=jnp.float32)
    d_rows_n, d_shift_a, d_scale_a = norm_back_a(d_normed_a)
    grad_tokens = (d_middle + d_rows_n).astype(jnp.bfloat16)
    d_per_token = jnp.concatenate(
        [d_shift_a, d_scale_a, d_gate_a, d_shift_m, d_scale_m, d_gate_m], axis=-1
    )
    d_modulation = jnp.einsum("stc,ste->sce", chooser, d_per_token, precision=lax.Precision.HIGHEST)
    grad_adaln = jnp.einsum(
        "scd,sce->de", cond_low.astype(jnp.float32), d_modulation, precision=lax.Precision.HIGHEST
    )
    grad_adaln_bias = jnp.sum(d_modulation, axis=(0, 1))
    (
        grad_query_bias,
        grad_value_bias,
        grad_output_bias,
        grad_up_bias,
        grad_down_bias,
        grad_adaln_bias,
        d_modulation,
    ) = (
        lax.psum(grad_query_bias.astype(jnp.bfloat16), "blk").astype(jnp.float32),
        lax.psum(grad_value_bias.astype(jnp.bfloat16), "blk").astype(jnp.float32),
        lax.psum(grad_output_bias.astype(jnp.bfloat16), "blk").astype(jnp.float32),
        lax.psum(grad_up_bias.astype(jnp.bfloat16), "blk").astype(jnp.float32),
        lax.psum(grad_down_bias.astype(jnp.bfloat16), "blk").astype(jnp.float32),
        lax.psum(grad_adaln_bias.astype(jnp.bfloat16), "blk").astype(jnp.float32),
        lax.psum(d_modulation.astype(jnp.bfloat16), "blk").astype(jnp.float32),
    )
    (
        grad_query_bias,
        grad_value_bias,
        grad_output_bias,
        grad_up_bias,
        grad_down_bias,
        grad_adaln_bias,
    ) = lax.psum(
        (
            grad_query_bias,
            grad_value_bias,
            grad_output_bias,
            grad_up_bias,
            grad_down_bias,
            grad_adaln_bias,
        ),
        "dp",
    )
    d_cond_act = jnp.einsum(
        "sce,de->scd",
        d_modulation,
        full_adaln,
        precision=lax.Precision.HIGHEST,
        preferred_element_type=jnp.float32,
    )
    grad_condition = silu_back(d_cond_act)[0]
    rowsum = (
        lax.psum_scatter(grad_qkv, "dp", scatter_dimension=0, tiled=True),
        lax.psum_scatter(grad_output, "dp", scatter_dimension=0, tiled=True),
        lax.psum_scatter(grad_up, "dp", scatter_dimension=0, tiled=True),
        lax.psum_scatter(grad_down, "dp", scatter_dimension=0, tiled=True),
        lax.psum_scatter(grad_adaln, "dp", scatter_dimension=0, tiled=True),
    )
    colsum = (
        lax.psum_scatter(
            rowsum[0].astype(jnp.bfloat16), "blk", scatter_dimension=1, tiled=True
        ).astype(jnp.float32),
        lax.psum_scatter(
            rowsum[1].astype(jnp.bfloat16), "blk", scatter_dimension=1, tiled=True
        ).astype(jnp.float32),
        lax.psum_scatter(
            rowsum[2].astype(jnp.bfloat16), "blk", scatter_dimension=1, tiled=True
        ).astype(jnp.float32),
        lax.psum_scatter(
            rowsum[3].astype(jnp.bfloat16), "blk", scatter_dimension=1, tiled=True
        ).astype(jnp.float32),
        lax.psum_scatter(
            rowsum[4].astype(jnp.bfloat16), "blk", scatter_dimension=1, tiled=True
        ).astype(jnp.float32),
    )
    shares = (
        lax.all_gather(colsum[0].astype(jnp.bfloat16), "blk", axis=1, tiled=True).astype(
            jnp.float32
        ),
        lax.all_gather(colsum[1].astype(jnp.bfloat16), "blk", axis=1, tiled=True).astype(
            jnp.float32
        ),
        lax.all_gather(colsum[2].astype(jnp.bfloat16), "blk", axis=1, tiled=True).astype(
            jnp.float32
        ),
        lax.all_gather(colsum[3].astype(jnp.bfloat16), "blk", axis=1, tiled=True).astype(
            jnp.float32
        ),
        lax.all_gather(colsum[4].astype(jnp.bfloat16), "blk", axis=1, tiled=True).astype(
            jnp.float32
        ),
    )
    return (
        output,
        grad_tokens,
        grad_condition,
        shares[0],
        grad_query_bias,
        grad_value_bias,
        shares[1],
        grad_output_bias,
        shares[2],
        grad_up_bias,
        shares[3],
        grad_down_bias,
        shares[4],
        grad_adaln_bias,
    )


def solution(mesh):
    in_specs = (
        P("dp", "blk", None),
        P("dp", None, None),
        P("dp", None),
        P("dp", None),
        P(),
        P(),
        P("dp", None),
        P(),
        P("dp", None),
        P(),
        P("dp", None),
        P(),
        P("dp", None),
        P(),
        P("dp", "blk", None),
    )
    out_specs = (
        P("dp", "blk", None),
        P("dp", "blk", None),
        P("dp", None, None),
        P("dp", None),
        P(),
        P(),
        P("dp", None),
        P(),
        P("dp", None),
        P(),
        P("dp", None),
        P(),
        P("dp", None),
        P(),
    )
    return jax.shard_map(
        per_device, mesh=mesh, in_specs=in_specs, out_specs=out_specs, check_vma=False
    )
```

profile of v0, /device:TPU:0, one launch (start us, length us, event | category | flops | bytes accessed | tf_op | source)
XLA Modules:
  0.0 2606.1 jit_solution(16766194997855355975)
XLA Ops:
  11.4 218.8 %all-gather.12.cloned.1.call-done = bf16[1152,6912]{1,0:T(8,128)(2,1)} async-done(((bf16[144,6912]{1,0:T(8,128)(2,1)}), bf16[1152,6912]{1,0:T(8,128)(2,1)}) %all-gather.12.cloned.1.call-update) | async-done | bytes 15925264 | tf_op jit(solution)/shard_map/all_gather | solution.py:63
  230.2 7.7 convolution_add_fusion
  237.9 3.0 convolution_bitcast_fusion
  240.9 3.0 copy-done
  244.3 105.9 %all-gather.14.cloned.1.call-done = bf16[1152,3456]{1,0:T(8,128)(2,1)} async-done(((bf16[144,3456]{1,0:T(8,128)(2,1)}), bf16[1152,3456]{1,0:T(8,128)(2,1)}) %all-gather.14.cloned.1.call-update) | async-done | bytes 7962640 | tf_op jit(solution)/shard_map/all_gather | solution.py:59
  350.2 5.8 fusion.3
  362.7 3.9 collective-permute-done
  366.6 6.3 collective-permute-done.1
  372.9 2.8 fusion.165
  375.7 3.7 select_reduce_fusion.3
  380.7 2.3 copy.121
  386.0 3.0 select_reduce_fusion.2
  392.5 2.9 select_reduce_fusion.1
  396.7 2.4 collective-permute-done.5
  404.2 3.9 fusion.15
  415.6 2.3 fusion.175
  417.9 4.3 fusion.170
  423.1 2.7 fusion.115
  425.9 132.8 %all-gather.18.cloned.1.call-done = bf16[1152,4608]{1,0:T(8,128)(2,1)} async-done(((bf16[144,4608]{1,0:T(8,128)(2,1)}), bf16[1152,4608]{1,0:T(8,128)(2,1)}) %all-gather.18.cloned.1.call-update) | async-done | bytes 10616848 | tf_op jit(solution)/shard_map/all_gather | solution.py:61
  558.7 9.5 convolution_add_fusion.1
  568.2 143.2 %all-gather.20.cloned.1.call-done = bf16[4608,1152]{1,0:T(8,128)(2,1)} async-done(((bf16[576,1152]{1,0:T(8,128)(2,1)}), bf16[4608,1152]{1,0:T(8,128)(2,1)}) %all-gather.20.cloned.1.call-update) | async-done | bytes 10616848 | tf_op jit(solution)/shard_map/all_gather | solution.py:62
  711.4 9.2 fusion.176
  722.0 8.7 fusion.178
  730.8 13.7 fusion.120
  745.5 8.4 multiply_reduce_fusion
  754.0 11.4 fusion.169
  774.8 4.3 multiply_convert_fusion.4
  796.6 7.7 collective-permute-done.7
  804.6 6.1 collective-permute-done.11
  811.7 5.3 collective-permute-done.8
  817.2 6.1 collective-permute-done.12
  825.5 4.1 collective-permute-done.9
  829.6 6.3 collective-permute-done.13
  835.9 6.7 constant_dynamic-update-slice_fusion.1
  847.3 3.0 fusion.174
  850.4 17.0 fusion.162
  868.6 3.2 fusion.117
  873.2 7.8 fusion.114
  881.1 195.1 %reduce-scatter.25.cloned.1.call-done = f32[144,4608]{1,0:T(8,128)} async-done(((f32[1152,4608]{1,0:T(8,128)}), f32[144,4608]{1,0:T(8,128)}) %reduce-scatter.25.cloned.1.call-update) | async-done | bytes 2654224 | tf_op jit(solution)/shard_map/reduce_scatter | solution.py:276
  1078.1 2.4 copy.183
  1080.6 346.5 %reduce-scatter.27.cloned.1.call-done = f32[576,1152]{1,0:T(8,128)} async-done(((f32[4608,1152]{1,0:T(8,128)}), f32[576,1152]{1,0:T(8,128)}) %reduce-scatter.27.cloned.1.call-update) | async-done | bytes 2654224 | tf_op jit(solution)/shard_map/reduce_scatter | solution.py:277
  1430.7 511.7 %reduce-scatter.29.cloned.1.call-done = f32[144,6912]{1,0:T(8,128)} async-done(((f32[1152,6912]{1,0:T(8,128)}), f32[144,6912]{1,0:T(8,128)}) %reduce-scatter.29.cloned.1.call-update) | async-done | bytes 3981328 | tf_op jit(solution)/shard_map/reduce_scatter | solution.py:278
  1942.4 2.3 convert_element_type.375
  1944.7 2.9 copy.187
  1948.3 101.0 %reduce-scatter.23.cloned.1.call-done = f32[144,1152]{1,0:T(8,128)} async-done(((f32[1152,1152]{1,0:T(8,128)}), f32[144,1152]{1,0:T(8,128)}) %reduce-scatter.23.cloned.1.call-update) | async-done | bytes 663568 | tf_op jit(solution)/shard_map/reduce_scatter | solution.py:275
  2051.6 270.5 %reduce-scatter.21.cloned.1.call-done = f32[144,3456]{1,0:T(8,128)} async-done(((f32[1152,3456]{1,0:T(8,128)}), f32[144,3456]{1,0:T(8,128)}) %reduce-scatter.21.cloned.1.call-update) | async-done | bytes 1990672 | tf_op jit(solution)/shard_map/reduce_scatter | solution.py:274
  2325.5 32.0 %reduce-scatter.35.cloned.1.call-done = bf16[1152,144]{1,0:T(8,128)(2,1)} async-done(((bf16[4608,144]{1,0:T(8,128)(2,1)}), bf16[1152,144]{1,0:T(8,128)(2,1)}) %reduce-scatter.35.cloned.1.call-update) | async-done | bytes 331792
  2359.6 28.5 %reduce-scatter.37.cloned.1.call-done = bf16[288,576]{1,0:T(8,128)(2,1)} async-done(((bf16[1152,576]{1,0:T(8,128)(2,1)}), bf16[288,576]{1,0:T(8,128)(2,1)}) %reduce-scatter.37.cloned.1.call-update) | async-done | bytes 331792
  2388.1 43.7 %reduce-scatter.39.cloned.1.call-done = bf16[1728,144]{1,0:T(8,128)(2,1)} async-done(((bf16[6912,144]{1,0:T(8,128)(2,1)}), bf16[1728,144]{1,0:T(8,128)(2,1)}) %reduce-scatter.39.cloned.1.call-update) | async-done | bytes 497680
  2431.8 2.2 copy.188
  2434.5 10.6 all-reduce.1
  2445.0 38.7 %all-reduce = (f32[1152]{0:T(1024)}, f32[1152]{0:T(1024)}, f32[1152]{0:T(1024)}, f32[4608]{0:T(1024)}, f32[1152]{0:T(1024)}, /*index=5*/f32[6912]{0:T(1024)}) all-reduce(bf16[1152]{0:T(1024)(128)(2,1)S(1)} %get-tuple-element.62, bf16[1152]{0:T(1024)(128)(2,1)S(1)} %get-tuple-element.63, ...), channel_id=1, replica_groups=mesh['dp'=8,'blk'=4] {'dp'}, use_global_device_ids=true, to_apply=%region_21.22 | all-reduce | flops 16128 | bytes 96768 | tf_op jit(solution)/shard_map/psum | solution.py:254
  2483.8 9.9 fusion.132
  2495.3 7.1 all-gather.1
  2503.8 19.3 reduce-scatter.31.cloned.1.call-done
  2524.4 9.8 all-gather
  2534.6 2.4 reshape.1028
  2537.0 6.5 all-gather.22.cloned.1.call-done
  2543.5 3.1 convert_element_type.370
  2546.6 17.5 all-gather.24.cloned.1.call-done
  2564.1 2.9 copy.151
  2567.0 21.6 all-gather.26.cloned.1.call-done
  2588.6 4.6 copy.149
  2593.2 5.9 reshape.1030
  (289 shorter events, 92.5 us)
Async XLA Ops:
  7.2 3.7 copy-start.9
  7.2 223.0 %copy-start.51 = (bf16[1,7,1152]{2,1,0:T(8,128)(2,1)S(1)}, bf16[1,7,1152]{2,1,0:T(8,128)(2,1)}, u32[]{:S(2)}) copy-start(bf16[1,7,1152]{2,1,0:T(8,128)(2,1)} %param.16) | copy-start | bytes 48388
  7.2 223.0 %all-gather.12.cloned.1.call-start = ((), (), s32[]{:S(2)}) async-start(), calls=%async_computation.10 | async-start | bytes 17915904 | tf_op jit(solution)/shard_map/all_gather | solution.py:63
  8.0 342.2 %all-gather.14.cloned.1.call-start = ((), (), s32[]{:S(2)}) async-start(), calls=%async_computation.11 | async-start | bytes 8957952 | tf_op jit(solution)/shard_map/all_gather | solution.py:59
  8.7 409.2 %all-gather.16.cloned.1.call-start = ((), (), s32[]{:S(2)}) async-start(), calls=%async_computation.12 | async-start | bytes 2985984 | tf_op jit(solution)/shard_map/all_gather | solution.py:60
  9.5 549.2 %all-gather.18.cloned.1.call-start = ((), (), s32[]{:S(2)}) async-start(), calls=%async_computation.13 | async-start | bytes 11943936 | tf_op jit(solution)/shard_map/all_gather | solution.py:61
  10.0 701.4 %all-gather.20.cloned.1.call-start = ((), (), s32[]{:S(2)}) async-start(), calls=%async_computation.14 | async-start | bytes 11943936 | tf_op jit(solution)/shard_map/all_gather | solution.py:62
  10.6 1065.6 %reduce-scatter.25.cloned.1.call-start = ((), (), s32[]{:S(2)}) async-start(), calls=%async_computation.18 | async-start | bytes 23887872 | tf_op jit(solution)/shard_map/reduce_scatter | solution.py:276
  11.4 226.5 %copy-start.63 = (f32[256]{0:T(256)}, f32[256]{0:T(256)S(1)}, u32[]{:S(2)}) copy-start(f32[256]{0:T(256)S(1)} %fusion.97) | copy-start | bytes 3076
  11.4 229.5 %copy-start.59 = (f32[256]{0:T(256)}, f32[256]{0:T(256)S(1)}, u32[]{:S(2)}) copy-start(f32[256]{0:T(256)S(1)} %fusion.137) | copy-start | bytes 3076
  244.2 111.7 %copy-start.30 = (bf16[256,1152]{1,0:T(8,128)(2,1)}, bf16[256,1152]{1,0:T(8,128)(2,1)S(1)}, u32[]{:S(2)}) copy-start(bf16[256,1152]{1,0:T(8,128)(2,1)S(1)} %fusion.116) | copy-start | bytes 1769476
  356.0 16.9 copy-start.10
  357.0 9.6 collective-permute-start
  357.0 15.9 collective-permute-start.1
  361.4 14.4 copy-start.15
  366.6 16.5 collective-permute-start.2
  372.9 12.6 collective-permute-start.3
  375.7 10.3 copy-start.38
  380.7 9.6 copy-start.13
  383.1 12.2 collective-permute-start.4
  385.6 13.5 collective-permute-start.5
  386.0 6.4 copy-start.36
  392.4 8.7 copy-start.34
  396.6 11.5 copy-start.11
  396.7 5.4 copy-start.40
  402.0 13.5 copy-start.7
  404.2 3.9 copy-start.5
  423.1 330.9 %copy-start.61 = (f32[256]{0:T(256)}, f32[256]{0:T(256)S(1)}, u32[]{:S(2)}) copy-start(f32[256]{0:T(256)S(1)} %fusion.138) | copy-start | bytes 3076
  711.4 10.6 copy-start.25
  730.7 696.3 %reduce-scatter.27.cloned.1.call-start = ((), (), s32[]{:S(2)}) async-start(), calls=%async_computation.20 | async-start | bytes 23887872 | tf_op jit(solution)/shard_map/reduce_scatter | solution.py:277
  744.5 1197.8 %reduce-scatter.29.cloned.1.call-start = ((), (), s32[]{:S(2)}) async-start(), calls=%async_computation.22 | async-start | bytes 35831808 | tf_op jit(solution)/shard_map/reduce_scatter | solution.py:278
  745.5 8.5 copy-start.66
  753.9 11.5 copy-start.17
  774.8 5.2 copy-start.2
  774.8 5.2 copy-start.32
  774.8 5.2 copy-start.41
  774.8 5.2 copy-start.55
  779.9 14.9 collective-permute-start.6
  780.9 14.7 collective-permute-start.10
  795.0 9.4 collective-permute-start.7
  795.7 14.9 collective-permute-start.11
  804.5 12.5 collective-permute-start.8
  810.8 12.5 collective-permute-start.12
  817.1 7.1 copy-start.12
  817.2 12.4 collective-permute-start.9
  823.5 12.5 collective-permute-start.13
  829.6 13.0 copy-start.42
  835.9 6.7 copy-start.28
  835.9 6.7 copy-start.64
  835.9 6.7 copy-start.60
  867.4 1181.9 %reduce-scatter.23.cloned.1.call-start = ((), (), s32[]{:S(2)}) async-start(), calls=%async_computation.17 | async-start | bytes 5971968 | tf_op jit(solution)/shard_map/reduce_scatter | solution.py:275
  871.9 1450.2 %reduce-scatter.21.cloned.1.call-start = ((), (), s32[]{:S(2)}) async-start(), calls=%async_computation.16 | async-start | bytes 17915904 | tf_op jit(solution)/shard_map/reduce_scatter | solution.py:274
  881.1 1476.4 %reduce-scatter.35.cloned.1.call-start = ((), (), s32[]{:S(2)}) async-start(), calls=%async_computation.26 | async-start | bytes 2949120
  1080.5 1307.5 %reduce-scatter.37.cloned.1.call-start = ((), (), s32[]{:S(2)}) async-start(), calls=%async_computation.27 | async-start | bytes 1843200
  1430.6 1001.2 %reduce-scatter.39.cloned.1.call-start = ((), (), s32[]{:S(2)}) async-start(), calls=%async_computation.28 | async-start | bytes 4423680
  1947.7 536.1 %all-reduce.4.cloned.1.call-start = ((), (), s32[]{:S(2)}) async-start(), calls=%async_computation.15 | async-start | bytes 221184 | tf_op jit(solution)/shard_map/psum | solution.py:245
  1948.2 546.1 %reduce-scatter.33.cloned.1.call-start = ((), (), s32[]{:S(2)}) async-start(), calls=%async_computation.25 | async-start | bytes 737280
  2051.5 471.7 %reduce-scatter.31.cloned.1.call-start = ((), (), s32[]{:S(2)}) async-start(), calls=%async_computation.24 | async-start | bytes 2211840
  2323.7 110.4 %copy-start.54 = (bf16[16,72]{1,0:T(8,128)(2,1)S(1)}, bf16[16,72]{1,0:T(8,128)(2,1)}, u32[]{:S(2)}) copy-start(bf16[16,72]{1,0:T(8,128)(2,1)} %get-tuple-element.124) | copy-start | bytes 6916
  2325.4 109.1 %copy-start.53 = (bf16[1152]{0:T(1024)(128)(2,1)S(1)}, bf16[1152]{0:T(1024)(128)(2,1)}, u32[]{:S(2)}) copy-start(bf16[1152]{0:T(1024)(128)(2,1)} %get-tuple-element.68) | copy-start | bytes 6916
  2325.4 109.1 %copy-start.57 = (bf16[4608]{0:T(1024)(128)(2,1)S(1)}, bf16[4608]{0:T(1024)(128)(2,1)}, u32[]{:S(2)}) copy-start(bf16[4608]{0:T(1024)(128)(2,1)} %get-tuple-element.126) | copy-start | bytes 27652
  2325.4 218.1 %all-gather.22.cloned.1.call-start = ((), (), s32[]{:S(2)}) async-start(), calls=%async_computation.19 | async-start | bytes 1658880 | tf_op jit(solution)/shard_map/all_gather | solution.py:304
  2359.5 204.5 %all-gather.24.cloned.1.call-start = ((), (), s32[]{:S(2)}) async-start(), calls=%async_computation.21 | async-start | bytes 1843200 | tf_op jit(solution)/shard_map/all_gather | solution.py:307
  2388.1 200.5 %all-gather.26.cloned.1.call-start = ((), (), s32[]{:S(2)}) async-start(), calls=%async_computation.23 | async-start | bytes 2580480 | tf_op jit(solution)/shard_map/all_gather | solution.py:310
  (42 other events, 89.8 us)
Sparse Core Ops, SparseCore 0:
  10.3 219.8 all-gather.11
  232.4 117.7 all-gather.13
  352.4 53.1 all-gather.15
  407.6 151.0 all-gather.17
  560.7 150.6 all-gather.19
  730.8 345.3 reduce-scatter.24
  1080.6 346.4 reduce-scatter.26
  1431.0 511.3 reduce-scatter.28
  1946.0 103.2 reduce-scatter.22
  2053.5 268.4 reduce-scatter.20
  2325.3 32.1 reduce-scatter.34
  2360.5 27.5 reduce-scatter.36
  2391.4 40.4 reduce-scatter.38
  2434.0 29.8 all-reduce.3
  2467.0 23.4 reduce-scatter.32
  2493.8 29.3 reduce-scatter.30
  2525.2 18.2 all-gather.21
  2544.9 19.0 all-gather.23
  2566.2 22.3 all-gather.25
where the time goes:
time: 2620 us; the launch traced here: 2610 us
  waiting for transfers between devices  2250 us (86%)
  matrix products  165 us (6%)
  local copies, waits for them, and re-layouts  67.8 us (3%)
  blocking collectives  66.1 us (3%)
  other arithmetic  35.9 us (1%)
    reduce_scatter x1, waiting for transfers between devices, per_device(): lax.psum_scatter(grad_adaln, 'dp', scatter_dimension=0, tiled=True)  512 us
    reduce_scatter x1, waiting for transfers between devices, per_device(): lax.psum_scatter(grad_down, 'dp', scatter_dimension=0, tiled=True)  346 us
    reduce_scatter x1, waiting for transfers between devices, per_device(): lax.psum_scatter(grad_qkv, 'dp', scatter_dimension=0, tiled=True)  270 us
    all_gather x1, waiting for transfers between devices, per_device(): lax.all_gather(adaln_weight, 'dp', axis=0, tiled=True)  219 us
    reduce_scatter x1, waiting for transfers between devices, per_device(): lax.psum_scatter(grad_up, 'dp', scatter_dimension=0, tiled=True)  195 us
    all_gather x1, waiting for transfers between devices, per_device(): lax.all_gather(down_weight, 'dp', axis=0, tiled=True)  143 us
    all_gather x1, waiting for transfers between devices, per_device(): lax.all_gather(up_weight, 'dp', axis=0, tiled=True)  133 us
    unnamed x24, waiting for transfers between devices  127 us
  transfers between devices with their start and end apart: 33, of which 27 were waited for; matrix products, arithmetic and copies ran while one was open for 9% of the time, Pallas kernels for 0%

commit v1 on v0

v1 whole, which is shorter than its diff:
```python
import functools
import math

import jax
import jax.numpy as jnp
from jax import lax
from jax.experimental import pallas as pl
from jax.experimental.pallas import tpu as pltpu
from jax.sharding import PartitionSpec as P

HEADS = 16
BLKS = 4
BF = jnp.bfloat16
F32 = jnp.float32
MESH = pl.DeviceIdType.MESH
EPS = 1e-06


def up_to(value, multiple):
    return -(-value // multiple) * multiple


def nn(a, b):
    return lax.dot_general(a, b, (((1,), (0,)), ((), ())), preferred_element_type=F32)


def nt(a, b):
    return lax.dot_general(a, b, (((1,), (1,)), ((), ())), preferred_element_type=F32)


def tn(a, b):
    return lax.dot_general(a, b, (((0,), (0,)), ((), ())), preferred_element_type=F32)


def exact(a, b):
    return lax.dot_general(
        a, b, (((1,), (0,)), ((), ())), precision=lax.Precision.HIGHEST, preferred_element_type=F32
    )


def unit_rows(rows):
    centre = rows - jnp.mean(rows, axis=-1, keepdims=True)
    inverse = lax.rsqrt(jnp.mean(centre * centre, axis=-1, keepdims=True) + EPS)
    return centre * inverse, inverse


def norm_back(grad, normed, inverse):
    mean_grad = jnp.mean(grad, axis=-1, keepdims=True)
    mean_both = jnp.mean(grad * normed, axis=-1, keepdims=True)
    return inverse * (grad - mean_grad - normed * mean_both)


def layer_kernel(dims, *refs):
    T, D, n, sub, R, Q, HD, hpd, F, Fr, MODW = dims
    L, C3, WH, nz = BLKS * T, 3 * Q, D // 2, n // 2
    CP = up_to(C3, 128)
    MQ = up_to(-(-MODW // BLKS), 256)
    WE, WL = up_to(5 * D, 1024), up_to(2 * D + 4 * up_to(Q, 128), 1024)
    QE, QL = WE // 4, WL // 4
    QP = up_to(Q, 128)
    factor = HD ** (-0.5)
    (
        x_in, cot_in, lab_col, lab_row, lab_own, cond_in, adaln_b, qkv_b, out_b, up_b, down_b,
        ad_h, wq_h, wo_h, wu_h, wd_h,
        out_o, gtok_o, dcond_o, ball_e, ball_l, gd_o, gu_o, gq_o, gw_o, na_h,
        wq, wo, wu, wd, ad, cond_rx, pm_tx, pm_rx, mod4, modf,
        na, dbm, act, gp, q3, lse, att_tx, att_rx, datt_tx, mid, bra,
        ps, rs_a, rs_b, gd, gu, gw, gd_x, gu_x, gq_x, gw_x, gd_z, gu_z, gq_z, gw_z,
        fin_d, fin_u, fin_q, fin_w, dk_acc, dv_acc, sb_e, sb_l, btx_e, btx_l, brx_e, brx_l, dc_tx,
        loc, g_s, g_r, c_s, c_r, p_s, p_r, m_s, m_r, ag_s, ag_r, a_s, a_r, r_s, r_r,
        x_s, x_r, z_s, z_r, f_s, f_r, b1_s, b1_r, b2_s, b2_r, b3_s, b3_r, d_s, d_r, w_s, w_r,
    ) = refs

    dp = lax.axis_index("dp")
    b = lax.axis_index("blk")
    g, member = dp // sub, dp % sub
    zi, xi = g // 2, g % 2
    core = b % 2
    b1, b2, b3 = b + 1 - 2 * core, (b + 2) % 4, 3 - b

    def rel(k):
        return ((b // 2 + k // 2) % 2) * 2 + (b % 2 + k % 2) % 2

    def at_dp(group):
        return (group * sub + member, b)

    def at_blk(index):
        return (dp, index)

    gx = g + 1 - 2 * xi

    def gz(k):
        return ((zi + k) % nz) * 2 + xi

    def remote(src, dst, ssem, rsem, where):
        return pltpu.make_async_remote_copy(
            src_ref=src, dst_ref=dst, send_sem=ssem, recv_sem=rsem, device_id=where, device_id_type=MESH
        )

    def strip(i):
        return pl.ds(pl.multiple_of(T * i, T), T)

    def rows_of(i, size):
        return pl.ds(pl.multiple_of(size * i, size), size)

    barrier = pltpu.get_barrier_semaphore()
    for k in range(1, n):
        pl.semaphore_signal(barrier, inc=1, device_id=at_dp((g + k) % n), device_id_type=MESH)
    for other in (b1, b2, b3):
        pl.semaphore_signal(barrier, inc=1, device_id=at_blk(other), device_id_type=MESH)
    pl.semaphore_wait(barrier, n - 1 + 3)

    cond_rx[g] = cond_in[g]
    cond_cp = [
        remote(cond_in.at[(g + k) % n], cond_rx.at[g], c_s.at[k], c_r.at[k], at_dp((g + k) % n))
        for k in range(1, n)
    ]
    for cp in cond_cp:
        cp.start()

    def place_q(i):
        return wq.at[rows_of(i, R), :]

    def place_o(i):
        return wo.at[core, rows_of(i, R), :]

    def place_u(i):
        return wu.at[rows_of(i, R), :]

    def place_d(i):
        return wd.at[rows_of(i, Fr), :]

    class Gather:
        def __init__(self, slot, src, place):
            self.src, self.place = src, place
            self.local = pltpu.make_async_copy(src, place(g), loc.at[slot])
            self.x0 = remote(src, place(g), g_s.at[slot, 0], g_r.at[slot, 0], at_dp(gx))
            self.z = {}
            self.x = {}
            for k in range(1, nz):
                self.z[k] = remote(src, place(g), g_s.at[slot, k], g_r.at[slot, k], at_dp(gz(k)))
                came = ((zi - k + nz) % nz) * 2 + xi
                self.x[k] = remote(
                    place(came), place(came), g_s.at[slot, nz + k], g_r.at[slot, nz + k], at_dp(gx)
                )

        def start(self):
            self.local.start()
            for k in list(range(2, nz)) + [1]:
                self.z[k].start()
            self.x0.start()

        def forward(self):
            for k in range(1, nz):
                self.z[k].wait_recv()
                self.x[k].start()

        def arrive(self):
            self.local.wait()
            self.x0.wait_recv()
            for k in range(1, nz):
                self.x[k].wait_recv()

        def done(self):
            self.x0.wait_send()
            for k in range(1, nz):
                self.z[k].wait_send()
                self.x[k].wait_send()

    take_q = Gather(0, wq_h, place_q)
    take_o = Gather(1, wo_h.at[core], place_o)
    take_u = Gather(2, wu_h, place_u)
    take_d = Gather(3, wd_h, place_d)
    start = pl.multiple_of(jnp.minimum(MQ * b, MODW - MQ), 128)
    ad_cp = pltpu.make_async_copy(ad_h.at[:, pl.ds(start, MQ)], ad, loc.at[4])
    ad_cp.start()
    take_q.start()

    for cp in cond_cp:
        cp.wait_recv()
    ad_cp.wait()
    cond_all = cond_rx[...].reshape(n * 8, R).astype(BF)
    partial = nn(cond_all, ad[...]).reshape(n, 8, MQ)
    halves = jnp.concatenate([partial[:, :, : MQ // 2], partial[:, :, MQ // 2 :]], axis=1)
    pm_tx[...] = halves.astype(BF)
    pm_rx[g] = pm_tx[g]
    part_cp = [
        remote(pm_tx.at[(g + k) % n], pm_rx.at[g], p_s.at[k], p_r.at[k], at_dp((g + k) % n))
        for k in range(1, n)
    ]
    for cp in part_cp:
        cp.start()
    rows_in = x_in[...].astype(F32)
    normed, _ = unit_rows(rows_in)
    for cp in part_cp:
        cp.wait_recv()
    total = jnp.sum(pm_rx[...].astype(F32), axis=0)
    own_mod = jnp.concatenate([total[:8], total[8:]], axis=1) + adaln_b[:, pl.ds(start, MQ)]
    mod4[b] = own_mod
    mod_cp = [
        remote(mod4.at[b], mod4.at[b], m_s.at[k], m_r.at[k], at_blk(rel(k))) for k in range(1, 4)
    ]
    for cp in mod_cp:
        cp.start()
    for cp in mod_cp:
        cp.wait_recv()
    for j in range(BLKS):
        first = min(MQ * j, MODW - MQ)
        skip = MQ * j - first
        modf[:, MQ * j : min(MQ * (j + 1), MODW)] = mod4[j][:, skip:]
    chooser = (lab_own[...] == lax.broadcasted_iota(jnp.int32, (T, 8), 1)).astype(F32)

    def per_token(piece):
        return exact(chooser, modf[:, D * piece : D * (piece + 1)])

    class Spread:
        def __init__(self, slot, buffer):
            def copy(index, src, where):
                return remote(
                    buffer.at[strip(src), :], buffer.at[strip(src), :], ag_s.at[slot, index], ag_r.at[slot, index],
                    at_blk(where),
                )

            self.near = copy(0, b, b1)
            self.far = copy(1, b, b2)
            self.onward = copy(2, b2, b1)

        def start(self):
            self.far.start()
            self.near.start()

        def forward(self):
            self.far.wait_recv()
            self.onward.start()

        def done(self):
            self.near.wait_send()
            self.far.wait_send()
            self.onward.wait_send()

    na[strip(b), :] = (normed * (1.0 + per_token(1)) + per_token(0)).astype(BF)
    spread_a = Spread(0, na)
    spread_a.start()
    upstream = cot_in[...].astype(F32)
    d_branch_m = (per_token(5) * upstream).astype(BF)
    dbm[strip(b), :] = d_branch_m
    sb_e[...] = jnp.zeros_like(sb_e)
    sb_l[...] = jnp.zeros_like(sb_l)
    sb_e[1:2, 4 * D : 5 * D] = jnp.sum(d_branch_m.astype(F32), axis=0, keepdims=True)
    take_o.start()
    take_u.start()
    take_q.forward()
    take_q.arrive()

    def project(k):
        i = rel(k)
        packed = nn(na[strip(i), :], wq[...]) + qkv_b[...]
        for s in range(3 * hpd):
            q3[s, strip(i), :] = packed[:, HD * s : HD * (s + 1)].astype(BF)

    def project_loop(lo, hi):
        def body(k, carry):
            project(k)
            return carry

        lax.fori_loop(lo, hi, body, 0)

    project_loop(0, 1)
    spread_a.near.wait_recv()
    project_loop(1, 2)
    spread_a.forward()
    project_loop(2, 3)
    spread_a.onward.wait_recv()
    project_loop(3, 4)
    keep_na = pltpu.make_async_copy(na, na_h, loc.at[5])
    keep_na.start()
    spread_d = Spread(1, dbm)
    spread_d.start()
    take_d.start()

    def attend(i):
        mask = lab_col[strip(i), :] == lab_row[...]
        pieces, logs = [], []
        for h in range(hpd):
            scores = nt(q3[h, strip(i), :], q3[hpd + h]) * factor
            scores = jnp.where(mask, scores, -1e30)
            top = jnp.max(scores, axis=-1, keepdims=True)
            raised = jnp.exp(scores - top)
            sums = jnp.sum(raised, axis=-1, keepdims=True)
            pieces.append(nn(raised.astype(BF), q3[2 * hpd + h]) / sums)
            logs.append(top + jnp.log(sums))
        att_tx[i] = jnp.concatenate(pieces, axis=1).astype(BF)
        lse[strip(i), :] = jnp.concatenate(logs, axis=1)

    att_cp = {
        k: remote(att_tx.at[rel(k)], att_rx.at[b], a_s.at[0, k], a_r.at[0, k], at_blk(rel(k)))
        for k in range(1, 4)
    }
    for turn, k in enumerate((2, 3, 1, 0)):
        attend(rel(k))
        if turn == 0:
            keep_na.wait()
            spread_a.done()
        if k:
            att_cp[k].start()
        if turn == 0:
            take_o.forward()
        if turn == 1:
            take_o.arrive()
            share_o = remote(wo.at[core], wo.at[core], g_s.at[1, 2 * nz], g_r.at[1, 2 * nz], at_blk(b1))
            share_o.start()
        if turn == 2:
            spread_d.forward()
    att_rx[b] = att_tx[b]
    take_u.forward()
    for k in range(1, 4):
        att_cp[k].wait_recv()
    share_o.wait_recv()
    attf = jnp.concatenate([att_rx[j] for j in range(BLKS)], axis=1)
    branch_a = jnp.concatenate([nn(attf, wo[0]), nn(attf, wo[1])], axis=1) + out_b[...]
    bra[...] = branch_a
    middle = rows_in_again(x_in) + per_token(2) * branch_a
    mid[...] = middle
    normed, _ = unit_rows(middle)
    na[strip(b), :] = (normed * (1.0 + per_token(4)) + per_token(3)).astype(BF)
    spread_m = Spread(2, na)
    spread_m.start()
    take_u.arrive()

    c0, c1 = math.sqrt(2.0 / math.pi), 0.044715

    def feed(k):
        i = rel(k)
        hidden = nn(na[strip(i), :], wu[...]) + up_b[...]
        square = hidden * hidden
        bent = jnp.tanh(c0 * (hidden + c1 * hidden * square))
        half = 0.5 * (1.0 + bent)
        act[strip(i), :] = (hidden * half).astype(BF)
        slope = half + 0.5 * hidden * (1.0 - bent * bent) * (c0 * (1.0 + (3.0 * c1) * square))
        gp[strip(i), :] = slope.astype(BF)

    def feed_down(k):
        i = rel(k)
        ps[i] = nn(act[strip(i), :], wd[...]).astype(BF)

    def loop(lo, hi, step):
        def body(k, carry):
            step(k)
            return carry

        lax.fori_loop(lo, hi, body, 0)

    class Reduce:
        def __init__(self, slot, rx):
            self.rx = rx
            self.near = remote(ps.at[b1], rx.at[0], r_s.at[slot, 0], r_r.at[slot, 0], at_blk(b1))
            self.pair = remote(ps.at[b3], rx.at[1], r_s.at[slot, 1], r_r.at[slot, 1], at_blk(b1))
            self.far = remote(ps.at[b2], rx.at[2], r_s.at[slot, 2], r_r.at[slot, 2], at_blk(b2))

        def cross(self):
            self.pair.wait_recv()
            ps[b2] = (ps[b2].astype(F32) + self.rx[1].astype(F32)).astype(BF)
            self.far.start()

        def result(self):
            self.near.wait_recv()
            self.far.wait_recv()
            total = ps[b].astype(F32) + self.rx[0].astype(F32) + self.rx[2].astype(F32)
            self.near.wait_send()
            self.pair.wait_send()
            self.far.wait_send()
            return total

    loop(0, 1, feed)
    spread_m.near.wait_recv()
    loop(1, 2, feed)
    take_d.forward()
    spread_m.forward()
    loop(2, 3, feed)
    spread_m.onward.wait_recv()
    loop(3, 4, feed)
    take_d.arrive()
    reduce_f = Reduce(0, rs_a)
    loop(3, 4, feed_down)
    reduce_f.pair.start()
    loop(2, 3, feed_down)
    reduce_f.cross()
    loop(1, 2, feed_down)
    reduce_f.near.start()
    loop(0, 1, feed_down)

    spread_d.near.wait_recv()
    spread_d.onward.wait_recv()

    class Scatter:
        def __init__(self, slot, grad, rows, xrx, zrx, fin, dest):
            cols = self.cols = fin.shape[1]
            self.slot, self.grad, self.rows, self.xrx, self.zrx, self.fin, self.dest = slot, grad, rows, xrx, zrx, fin, dest
            self.x, self.z = {}, {}
            for k in range(nz):
                z_at = (zi + k) % nz
                self.x[k] = remote(
                    grad.at[rows_of(2 * z_at + 1 - xi, rows), pl.ds(0, cols)], xrx.at[z_at],
                    x_s.at[slot, k], x_r.at[slot, k], at_dp(gx),
                )
                if k:
                    self.z[k] = remote(
                        xrx.at[z_at], zrx.at[nz - k - 1], z_s.at[slot, k], z_r.at[slot, nz - k], at_dp(gz(k))
                    )
            self.local = pltpu.make_async_copy(fin, dest.at[b], loc.at[6 + slot])
            self.near = remote(fin, dest.at[b], f_s.at[slot, 0], f_r.at[slot, 0], at_blk(b1))
            self.far = remote(fin, dest.at[b], f_s.at[slot, 1], f_r.at[slot, 1], at_blk(b2))
            self.onward = remote(dest.at[b2], dest.at[b2], f_s.at[slot, 2], f_r.at[slot, 2], at_blk(b1))

        def start(self):
            for k in list(range(1, nz)) + [0]:
                self.x[k].start()

        def cross(self):
            for k in range(1, nz):
                z_at = (zi + k) % nz
                self.x[k].wait_recv()
                own = self.grad[rows_of(2 * z_at + xi, self.rows), 0 : self.cols].astype(F32)
                self.xrx[z_at] = (own + self.xrx[z_at].astype(F32)).astype(BF)
                self.z[k].start()

        def total(self):
            self.x[0].wait_recv()
            own = self.grad[rows_of(g, self.rows), 0 : self.cols].astype(F32) + self.xrx[zi].astype(F32)
            for k in range(1, nz):
                remote(
                    self.xrx.at[0], self.zrx.at[k - 1], z_s.at[0, 0], z_r.at[self.slot, k], at_dp(gx)
                ).wait_recv()
                own = own + self.zrx[k - 1].astype(F32)
            self.fin[...] = own.astype(BF)
            self.far.start()
            self.near.start()
            self.local.start()

        def forward(self):
            self.far.wait_recv()
            self.onward.start()

        def done(self):
            self.near.wait_recv()
            self.onward.wait_recv()
            self.local.wait()
            self.near.wait_send()
            self.far.wait_send()
            self.onward.wait_send()
            for k in range(nz):
                self.x[k].wait_send()
                if k:
                    self.z[k].wait_send()


    give_d = Scatter(0, gd, Fr, gd_x, gd_z, fin_d, gd_o)
    give_u = Scatter(1, gu, R, gu_x, gu_z, fin_u, gu_o)
    give_q = Scatter(2, wu, R, gq_x, gq_z, fin_q, gq_o)

    def hidden_back(k):
        i = rel(k)
        d_active = nt(dbm[strip(i), :], wd[...])
        gp[strip(i), :] = (gp[strip(i), :].astype(F32) * d_active).astype(BF)

    def tiles(size):
        return 384 if size % 384 == 0 else size

    def weight_grad(dest, left, right, size):
        step = tiles(size)

        def body(j, carry):
            at = pl.ds(pl.multiple_of(step * j, step), step)
            dest[at, :] = tn(left[:, at], right[...]).astype(BF)
            return carry

        lax.fori_loop(0, size // step, body, 0)

    loop(0, 4, hidden_back)
    weight_grad(gd, act, dbm, F)
    give_d.start()
    weight_grad(gu, na, gp, D)
    give_u.start()
    at_e7 = pl.ds(pl.multiple_of(F * b, 128), F)

    one_hot = (lax.broadcasted_iota(jnp.int32, (8, T), 0) == lab_row[:, strip(b)]).astype(F32)

    def per_crop(values):
        return exact(one_hot, values)

    branch_m = reduce_f.result() + down_b[...]
    out_o[...] = (mid[...] + per_token(5) * branch_m).astype(BF)
    sb_e[:, 3 * D : 4 * D] = per_crop(cot_in[...].astype(F32) * branch_m)

    def up_back(k):
        i = rel(k)
        ps[i] = nt(gp[strip(i), :], wu[...]).astype(BF)

    spread_d.done()
    reduce_m = Reduce(1, rs_b)
    loop(3, 4, up_back)
    reduce_m.pair.start()
    loop(2, 3, up_back)
    reduce_m.cross()
    loop(1, 2, up_back)
    reduce_m.near.start()
    loop(0, 1, up_back)
    na_back = pltpu.make_async_copy(na_h, na, loc.at[5])
    spread_m.done()
    na_back.start()
    up_sums = jnp.sum(gp[...].astype(F32), axis=0, keepdims=True)
    give_d.cross()
    d_normed = reduce_m.result()
    normed, inverse = unit_rows(mid[...])
    d_middle = cot_in[...].astype(F32) + norm_back(d_normed * (1.0 + per_token(4)), normed, inverse)
    mid[...] = d_middle
    d_branch_a = (per_token(2) * d_middle).astype(BF)

    d_att = (nt(d_branch_a[:, :WH], wo[0]) + nt(d_branch_a[:, WH:], wo[1])).astype(BF)
    for j in range(BLKS):
        datt_tx[j] = d_att[:, Q * j : Q * (j + 1)]
    datt_cp = {
        k: remote(datt_tx.at[rel(k)], att_rx.at[b], a_s.at[1, k], a_r.at[1, k], at_blk(rel(k)))
        for k in range(1, 4)
    }
    for k in (2, 3, 1):
        datt_cp[k].start()
    dbm[strip(b), :] = d_branch_a
    spread_w = Spread(3, dbm)
    spread_w.start()
    att_rx[b] = datt_tx[b]
    sb_e[:, 0:D] = per_crop(d_middle * bra[...])
    sb_e[:, D : 2 * D] = per_crop(d_normed)
    sb_e[:, 2 * D : 3 * D] = per_crop(d_normed * normed)
    sb_e[7:8, at_e7] = up_sums
    sb_e[0:1, 4 * D : 5 * D] = jnp.sum(d_branch_a.astype(F32), axis=0, keepdims=True)

    class Bundle:
        def __init__(self, slot, sums, tx, rx, ball, quarter):
            self.sums, self.tx, self.rx, self.ball, self.quarter = sums, tx, rx, ball, quarter
            self.one = [
                remote(tx.at[rel(k)], rx.at[b], b1_s.at[slot, k], b1_r.at[slot, k], at_blk(rel(k)))
                for k in range(1, 4)
            ]
            self.two = [
                remote(ball.at[b, g], ball.at[b, g], b2_s.at[slot, k], b2_r.at[slot, k], at_dp((g + k) % n))
                for k in range(1, n)
            ]
            self.three = [
                remote(ball.at[b], ball.at[b], b3_s.at[slot, k], b3_r.at[slot, k], at_blk(rel(k)))
                for k in range(1, 4)
            ]

        def start(self):
            half = self.quarter // 2
            for j in range(BLKS):
                first = self.sums[:, 2 * half * j : 2 * half * j + half]
                second = self.sums[:, 2 * half * j + half : 2 * half * (j + 1)]
                self.tx[j] = jnp.concatenate([first, second], axis=0).astype(BF)
            self.rx[b] = self.tx[b]
            for cp in self.one:
                cp.start()

        def groups(self):
            for cp in self.one:
                cp.wait_recv()
            self.ball[b, g] = jnp.sum(self.rx[...].astype(F32), axis=0).astype(BF)
            for cp in self.two:
                cp.start()

        def share(self):
            for cp in self.two:
                cp.wait_recv()
            for cp in self.three:
                cp.start()

        def arrive(self):
            for cp in self.three:
                cp.wait_recv()

        def done(self):
            for cp in self.one + self.two + self.three:
                cp.wait_send()

    bundle_e = Bundle(0, sb_e, btx_e, brx_e, ball_e, QE)
    bundle_l = Bundle(1, sb_l, btx_l, brx_l, ball_l, QL)
    bundle_e.start()
    for k in range(1, 4):
        datt_cp[k].wait_recv()

    def head_back(h):
        dk_acc[...] = jnp.zeros_like(dk_acc)
        dv_acc[...] = jnp.zeros_like(dv_acc)

        def body(i, carry):
            at = strip(i)
            query, keys, values = q3[h, at, :], q3[hpd + h], q3[2 * hpd + h]
            mask = lab_col[at, :] == lab_row[...]
            scores = jnp.where(mask, nt(query, keys) * factor, -1e30)
            probs = jnp.exp(scores - lse[at, h : h + 1])
            d_out = att_rx[i, :, HD * h : HD * (h + 1)]
            kept = att_tx[i, :, HD * h : HD * (h + 1)]
            delta = jnp.sum(d_out.astype(F32) * kept.astype(F32), axis=-1, keepdims=True)
            dv_acc[...] += tn(probs.astype(BF), d_out)
            d_scores = (probs * (nt(d_out, values) - delta)).astype(BF)
            dk_acc[...] += tn(d_scores, query)
            q3[h, at, :] = (nn(d_scores, keys) * factor).astype(BF)
            return carry

        lax.fori_loop(0, BLKS, body, 0)
        q3[hpd + h] = (dk_acc[...] * factor).astype(BF)
        q3[2 * hpd + h] = dv_acc[...].astype(BF)

    class OutScatter:
        def __init__(self):
            self.x = remote(gw.at[rows_of(1 - xi, R), :], gw_x, w_s.at[0], w_r.at[0], at_dp(gx))
            at = jnp.maximum((zi - b + nz) % nz, 1) - 1
            self.z = remote(gw_x, gw_z.at[at], w_s.at[1], w_r.at[1 + at], at_dp(2 * b + xi))
            self.local = pltpu.make_async_copy(fin_w, gw_o, loc.at[9])
            self.out = [
                remote(fin_w, gw_o, w_s.at[1 + k], w_r.at[nz + 1], at_blk(rel(k))) for k in range(1, 4)
            ]

        def start(self):
            self.x.start()

        def cross(self):
            self.x.wait_recv()
            total = gw[rows_of(xi, R), :].astype(F32) + gw_x[...].astype(F32)
            gw_x[...] = total.astype(BF)

            @pl.when(zi != b)
            def _():
                self.z.start()

        def total(self):
            @pl.when(zi == b)
            def _():
                own = gw_x[...].astype(F32)
                for k in range(1, nz):
                    remote(gw_x, gw_z.at[k - 1], w_s.at[0], w_r.at[k], at_dp(gx)).wait_recv()
                    own = own + gw_z[k - 1].astype(F32)
                fin_w[...] = own.astype(BF)
                for cp in self.out:
                    cp.start()
                self.local.start()

        def done(self):
            self.x.wait_send()

            @pl.when(zi != b)
            def _():
                self.z.wait_send()
                self.out[0].wait_recv()

            @pl.when(zi == b)
            def _():
                for cp in self.out:
                    cp.wait_send()
                self.local.wait()

    take_d.done()
    pieces_cp = [
        pltpu.make_async_copy(ad_h.at[:, pl.ds(D * p, D)], wd.at[pl.ds(R * p, R), pl.ds(0, D)], loc.at[10 + p])
        for p in range(6)
    ]
    for cp in pieces_cp:
        cp.start()
    give_w = OutScatter()
    head_back(0)
    give_d.total()
    give_u.cross()
    bundle_e.groups()
    spread_w.forward()
    head_back(1)
    bundle_e.share()
    spread_w.near.wait_recv()
    spread_w.onward.wait_recv()
    att_all = att_tx[...].reshape(L, Q)
    gw[...] = tn(att_all, dbm[...]).astype(BF)
    give_w.start()
    give_d.forward()
    head_back(2)
    give_u.total()
    give_w.cross()
    head_back(3)
    give_u.forward()
    give_w.total()

    def back_rows(i):
        return jnp.concatenate([q3[s, strip(i), :] for s in range(3 * hpd)], axis=1)

    def qkv_back(k):
        i = rel(k)
        d_packed = back_rows(i)
        act[strip(i), 0:C3] = d_packed
        ps[i] = nt(d_packed, wq[...]).astype(BF)

    reduce_a = Reduce(2, rs_a)
    loop(3, 4, qkv_back)
    reduce_a.pair.start()
    loop(2, 3, qkv_back)
    reduce_a.cross()
    loop(1, 2, qkv_back)
    reduce_a.near.start()
    loop(0, 1, qkv_back)
    na_back.wait()
    take_u.done()
    step = tiles(D)

    def grad_body(j, carry):
        at = pl.ds(pl.multiple_of(step * j, step), step)
        wu[at, 0:C3] = tn(na[:, at], act[:, 0:C3]).astype(BF)
        return carry

    lax.fori_loop(0, D // step, grad_body, 0)
    give_q.start()
    bias_sums = jnp.sum(act[:, 0:C3].astype(F32), axis=0, keepdims=True)
    pad = jnp.zeros((1, QP - Q), F32)
    at_l = pl.ds(pl.multiple_of(2 * D + QP * b, 128), QP)
    sb_l[0:1, at_l] = jnp.concatenate([bias_sums[:, :Q], pad], axis=1)
    sb_l[1:2, at_l] = jnp.concatenate([bias_sums[:, 2 * Q :], pad], axis=1)
    d_normed = reduce_a.result()
    normed, inverse = unit_rows(rows_in_again(x_in))
    sb_l[:, 0:D] = per_crop(d_normed)
    sb_l[:, D : 2 * D] = per_crop(d_normed * normed)
    bundle_l.start()
    gtok_o[...] = (mid[...] + norm_back(d_normed * (1.0 + per_token(1)), normed, inverse)).astype(BF)
    bundle_l.groups()
    give_q.cross()
    bundle_e.arrive()
    for cp in pieces_cp:
        cp.wait()

    def crop_part(ball, j, columns, half, first, width):
        both = ball[j].astype(F32)
        rows = both[:, 0:8, :] if half == 0 else both[:, 8:16, :]
        rows = rows.reshape(n * 8, columns).astype(BF)
        total, at = 0.0, first
        while at < first + width:
            p = at // D
            end = min(first + width, D * (p + 1))
            total = total + nt(rows[:, at - first : end - first], wd[R * p : R * (p + 1), at - D * p : end - D * p])
            at = end
        return total

    d_cond = jnp.zeros((n * 8, R), F32)
    for j in range(BLKS):
        for half in range(2):
            first = QE * j + half * (QE // 2)
            width = min(QE // 2, 4 * D - first)
            if width > 0:
                d_cond = d_cond + crop_part(ball_e, j, QE // 2, half, 2 * D + first, width)
    bundle_l.share()
    bundle_l.arrive()
    for j in range(BLKS):
        for half in range(2):
            first = QL * j + half * (QL // 2)
            width = min(QL // 2, 2 * D - first)
            if width > 0:
                d_cond = d_cond + crop_part(ball_l, j, QL // 2, half, first, width)
    dc_tx[...] = d_cond.reshape(n, 8, R)
    dcond_o[g] = dc_tx[g]
    dcond_cp = [
        remote(dc_tx.at[(g + k) % n], dcond_o.at[g], d_s.at[k], d_r.at[k], at_dp((g + k) % n))
        for k in range(1, n)
    ]
    for cp in dcond_cp:
        cp.start()
    give_q.total()
    give_q.forward()
    for cp in dcond_cp:
        cp.wait_recv()

    give_q.done()
    give_d.done()
    give_u.done()
    give_w.done()
    bundle_e.done()
    bundle_l.done()
    for cp in cond_cp + part_cp + mod_cp + dcond_cp:
        cp.wait_send()
    for k in range(1, 4):
        att_cp[k].wait_send()
        datt_cp[k].wait_send()
    spread_w.done()
    share_o.wait_send()
    for take in (take_q, take_o):
        take.done()


def rows_in_again(x_in):
    return x_in[...].astype(F32)


def run_layer(dims, inputs, n_out):
    T, D, n, sub, R, Q, HD, hpd, F, Fr, MODW = dims
    L, C3, WH, nz = BLKS * T, 3 * Q, D // 2, n // 2
    CP = up_to(C3, 128)
    MQ = up_to(-(-MODW // BLKS), 256)
    WE, WL = up_to(5 * D, 1024), up_to(2 * D + 4 * up_to(Q, 128), 1024)
    vm = pl.BlockSpec(memory_space=pltpu.VMEM)
    hbm = pl.BlockSpec(memory_space=pl.ANY)
    out_shape = (
        jax.ShapeDtypeStruct((T, D), BF),
        jax.ShapeDtypeStruct((T, D), BF),
        jax.ShapeDtypeStruct((n, 8, R), F32),
        jax.ShapeDtypeStruct((BLKS, n, 16, WE // 8), BF),
        jax.ShapeDtypeStruct((BLKS, n, 16, WL // 8), BF),
        jax.ShapeDtypeStruct((BLKS, Fr, D), BF),
        jax.ShapeDtypeStruct((BLKS, R, F), BF),
        jax.ShapeDtypeStruct((BLKS, R, CP), BF),
        jax.ShapeDtypeStruct((R, D), BF),
        jax.ShapeDtypeStruct((L, D), BF),
    )
    dma = pltpu.SemaphoreType.DMA
    scratch = [
        pltpu.VMEM((D, C3), BF),
        pltpu.VMEM((2, D, WH), BF),
        pltpu.VMEM((D, F), BF),
        pltpu.VMEM((F, D), BF),
        pltpu.VMEM((R, MQ), BF),
        pltpu.VMEM((n, 8, R), F32),
        pltpu.VMEM((n, 16, MQ // 2), BF),
        pltpu.VMEM((n, 16, MQ // 2), BF),
        pltpu.VMEM((BLKS, 8, MQ), F32),
        pltpu.VMEM((8, MODW), F32),
        pltpu.VMEM((L, D), BF),
        pltpu.VMEM((L, D), BF),
        pltpu.VMEM((L, F), BF),
        pltpu.VMEM((L, F), BF),
        pltpu.VMEM((3 * hpd, L, HD), BF),
        pltpu.VMEM((L, hpd), F32),
        pltpu.VMEM((BLKS, T, Q), BF),
        pltpu.VMEM((BLKS, T, Q), BF),
        pltpu.VMEM((BLKS, T, Q), BF),
        pltpu.VMEM((T, D), F32),
        pltpu.VMEM((T, D), F32),
        pltpu.VMEM((BLKS, T, D), BF),
        pltpu.VMEM((3, T, D), BF),
        pltpu.VMEM((3, T, D), BF),
        pltpu.VMEM((F, D), BF),
        pltpu.VMEM((D, F), BF),
        pltpu.VMEM((Q, D), BF),
        pltpu.VMEM((nz, Fr, D), BF),
        pltpu.VMEM((nz, R, F), BF),
        pltpu.VMEM((nz, R, CP), BF),
        pltpu.VMEM((R, D), BF),
        pltpu.VMEM((nz - 1, Fr, D), BF),
        pltpu.VMEM((nz - 1, R, F), BF),
        pltpu.VMEM((nz - 1, R, CP), BF),
        pltpu.VMEM((nz - 1, R, D), BF),
        pltpu.VMEM((Fr, D), BF),
        pltpu.VMEM((R, F), BF),
        pltpu.VMEM((R, CP), BF),
        pltpu.VMEM((R, D), BF),
        pltpu.VMEM((L, HD), F32),
        pltpu.VMEM((L, HD), F32),
        pltpu.VMEM((8, WE), F32),
        pltpu.VMEM((8, WL), F32),
        pltpu.VMEM((BLKS, 16, WE // 8), BF),
        pltpu.VMEM((BLKS, 16, WL // 8), BF),
        pltpu.VMEM((BLKS, 16, WE // 8), BF),
        pltpu.VMEM((BLKS, 16, WL // 8), BF),
        pltpu.VMEM((n, 8, R), F32),
        dma((16,)),
        dma((4, 2 * nz + 1)), dma((4, 2 * nz + 1)),
        dma((n,)), dma((n,)), dma((n,)), dma((n,)),
        dma((4,)), dma((4,)),
        dma((4, 3)), dma((4, 3)),
        dma((2, 4)), dma((2, 4)),
        dma((3, 3)), dma((3, 3)),
        dma((3, nz)), dma((3, nz)), dma((3, nz)), dma((3, nz)),
        dma((3, 3)), dma((3, 3)),
        dma((2, 4)), dma((2, 4)), dma((2, n)), dma((2, n)), dma((2, 4)), dma((2, 4)),
        dma((n,)), dma((n,)),
        dma((nz + 2,)), dma((nz + 2,)),
    ]
    in_specs = [vm] * 11 + [hbm] * 5
    out_specs = [vm] * 5 + [hbm] * 5
    return pl.pallas_call(
        functools.partial(layer_kernel, dims),
        out_shape=out_shape,
        in_specs=in_specs,
        out_specs=out_specs,
        scratch_shapes=scratch,
        compiler_params=pltpu.CompilerParams(
            collective_id=0, has_side_effects=True, vmem_limit_bytes=63 << 20
        ),
        name="layer",
    )(*inputs)


def per_device(sub, tokens, condition, segment_ids, qkv_weight, query_bias, value_bias, output_weight, output_bias,
               up_weight, up_bias, down_weight, down_bias, adaln_weight, adaln_bias, cotangent):
    T, D = tokens.shape[1:]
    blks, size = lax.axis_size("blk"), lax.axis_size("dp")
    assert blks == BLKS and tokens.shape[0] == 1
    n = size // sub
    HD = D // HEADS
    hpd = HEADS // blks
    Q = D // blks
    FF = up_weight.shape[1]
    MODW = adaln_weight.shape[1]
    F = FF // blks
    R, Fr = D // n, F // n
    b = lax.axis_index("blk")
    dp = lax.axis_index("dp")

    def members(step):
        return [(i, i - i % sub + (i + step) % sub) for i in range(size)]

    def collect(w):
        if sub == 1:
            return w
        full = jnp.zeros((sub,) + w.shape, w.dtype)
        for step in range(sub):
            moved = lax.ppermute(w, "dp", members(step)) if step else w
            full = lax.dynamic_update_index_in_dim(full, moved, (dp - step) % sub, 0)
        return full.reshape((-1,) + w.shape[1:])

    def settle(grad):
        if sub == 1:
            return grad
        parts = grad.reshape((sub, -1) + grad.shape[1:])
        total = 0.0
        for step in range(sub):
            part = lax.dynamic_index_in_dim(parts, (dp + step) % sub, 0, keepdims=False)
            total = total + (lax.ppermute(part, "dp", members(step)) if step else part)
        return total

    def over_members(vector):
        if sub == 1:
            return vector
        total = vector
        for step in range(1, sub):
            total = total + lax.ppermute(vector, "dp", members(step))
        return total

    def pick(w, groups, width):
        return lax.dynamic_index_in_dim(w.reshape(w.shape[0], groups, blks, width), b, 2, keepdims=False).reshape(
            w.shape[0], groups * width
        )

    qkv_own = pick(collect(qkv_weight), 3, Q)
    out_own = collect(output_weight).reshape(R, 2, D // 2).transpose(1, 0, 2)
    up_own = pick(collect(up_weight), n, Fr)
    down_own = lax.dynamic_slice_in_dim(collect(down_weight), b * Fr, Fr, 0)
    adaln_own = collect(adaln_weight)
    qkv_bias = jnp.concatenate([query_bias, jnp.zeros_like(query_bias), value_bias]).astype(F32)[None]
    crops = condition.shape[1]
    cond = condition[0].astype(F32)
    cond_act, silu_back = jax.vjp(jax.nn.silu, cond)
    cond_low = cond_act.astype(BF).astype(F32)
    cond_rows = jnp.pad(cond_low, ((0, 8 - crops), (0, 0))).reshape(8, n, R).transpose(1, 0, 2)
    own_labels = lax.dynamic_slice_in_dim(segment_ids, b * T, T, 1)
    inputs = (
        tokens[0], cotangent[0], segment_ids.reshape(-1, 1), segment_ids, own_labels.reshape(T, 1), cond_rows,
        adaln_bias.astype(F32)[None], pick(qkv_bias, 3, Q), output_bias.astype(F32)[None],
        pick(up_bias.astype(F32)[None], n, Fr), down_bias.astype(F32)[None],
        adaln_own, qkv_own, out_own, up_own, down_own,
    )
    dims = (T, D, n, sub, R, Q, HD, hpd, F, Fr, MODW)
    out, gtok, dcond, ball_e, ball_l, gd, gu, gq, gw, _ = run_layer(dims, inputs, 10)

    def crops_of(ball):
        half = ball.shape[-1]
        return ball.reshape(blks, n, 2, 8, half).transpose(1, 3, 0, 2, 4).reshape(n, 8, blks * 2 * half).astype(F32)

    early, late = crops_of(ball_e), crops_of(ball_l)
    QP = up_to(Q, 128)
    d_mod = jnp.concatenate([late[:, :crops, : 2 * D], early[:, :crops, : 4 * D]], axis=-1)
    cond_all = cond_rows_all(cond_low, n, sub, members, dp, R, crops)
    grad_adaln = jnp.einsum("scd,sce->de", cond_all.astype(BF), d_mod.astype(BF), preferred_element_type=F32)
    early_sum, late_sum = over_members(jnp.sum(early, axis=0)), over_members(jnp.sum(late, axis=0))
    grad_adaln_bias = over_members(jnp.sum(d_mod, axis=(0, 1)))
    grad_output_bias = early_sum[0, 4 * D : 5 * D]
    grad_down_bias = early_sum[1, 4 * D : 5 * D]
    grad_up_bias = early_sum[7, :FF].reshape(blks, n, Fr).transpose(1, 0, 2).reshape(FF)
    slots = late_sum[:2, 2 * D : 2 * D + 4 * QP].reshape(2, blks, QP)[:, :, :Q].reshape(2, D)
    d_cond_act = dcond.transpose(1, 0, 2).reshape(8, D)[:crops]
    grad_condition = silu_back(d_cond_act)[0][None]
    grad_qkv = gq[:, :, : 3 * Q].astype(F32).reshape(blks, R, 3, Q).transpose(1, 2, 0, 3).reshape(R, 3 * D)
    grad_up = gu.astype(F32).reshape(blks, R, n, Fr).transpose(1, 2, 0, 3).reshape(R, FF)
    grad_down = gd.astype(F32).reshape(blks * Fr, D)
    return (
        out[None], gtok[None], grad_condition, settle(grad_qkv), slots[0], slots[1], settle(gw.astype(F32)),
        grad_output_bias, settle(grad_up), grad_up_bias, settle(grad_down), grad_down_bias, settle(grad_adaln),
        grad_adaln_bias,
    )


def cond_rows_all(cond_low, n, sub, members, dp, R, crops):
    size = n * sub
    g = dp // sub
    blocks = cond_low.reshape(crops, n, R).transpose(1, 0, 2)
    full = jnp.zeros((n, crops, R), F32)
    for step in range(n):
        part = lax.dynamic_index_in_dim(blocks, (g + step) % n, 0, keepdims=False)
        perm = [(i, ((i // sub + step) % n) * sub + i % sub) for i in range(size)]
        moved = lax.ppermute(part, "dp", perm) if step else part
        full = lax.dynamic_update_index_in_dim(full, moved, (g - step) % n, 0)
    return full


def solution(mesh):
    rows, strips = P("dp", None), P("dp", "blk", None)
    in_specs = (
        strips, P("dp", None, None), rows, rows, P(), P(), rows, P(), rows, P(), rows, P(), rows, P(), strips,
    )
    out_specs = (
        strips, strips, P("dp", None, None), rows, P(), P(), rows, P(), rows, P(), rows, P(), rows, P(),
    )

    def whole(*args):
        size = mesh.shape["dp"]
        rows_each = args[3].shape[0] // size
        sub = 1
        while (rows_each * sub) % 16:
            sub *= 2
        body = functools.partial(per_device, sub)
        return jax.shard_map(body, mesh=mesh, in_specs=in_specs, out_specs=out_specs, check_vma=False)(*args)

    return whole
```

time: 2620 us -> 436 us (0.17)
  waiting for transfers between devices: 2250 us -> 0.02 us
  Pallas kernels: 0 us -> 331 us
  matrix products: 165 us -> 2.66 us
  blocking collectives: 66.1 us -> 0 us
  other arithmetic: 35.9 us -> 7.18 us
    reduce_scatter x5 -> x0, waiting for transfers between devices: 1420 us -> none  [the longest x1 512 us: per_device(): lax.psum_scatter(grad_adaln, 'dp', scatter_dimension=0, tiled=True)]
    all_gather x8 -> x0, waiting for transfers between devices: 646 us -> none  [the longest x1 219 us: per_device(): lax.all_gather(adaln_weight, 'dp', axis=0, tiled=True)]
    pallas_call x0 -> x1, Pallas kernels: none -> 331 us  [run_layer(): pl.pallas_call(functools.partial(layer_kernel, dims), out_shape=out_shape...]
    dot_general x41 -> x1, matrix products: 165 us -> 2.66 us  [per_device(): jnp.einsum('scd,sce->de', cond_all.astype(BF), d_mod.astype(BF), preferre...]
    unnamed x24 -> x0, waiting for transfers between devices: 127 us -> none
    ppermute x14 -> x7, waiting for transfers between devices: 49.7 us -> 0.02 us  [cond_rows_all(): moved = lax.ppermute(part, 'dp', perm) if step else part]
    psum x2 -> x0, blocking collectives: 49.3 us -> none  [the longest x1 38.7 us: per_device(): lax.psum((grad_query_bias, grad_value_bias, grad_output_bias, grad_up_bia...]
    reshape x0 -> x19, local copies, waits for them, and re-layouts: none -> 45.2 us  [the longest x3 19.3 us: per_device(): gu.astype(F32).reshape(blks, R, n, Fr).transpose(1, 2, 0, 3).reshape(R, FF)]
  transfers between devices with their start and end apart: 33 -> 7, of which waited for: 27 -> 0; matrix products, arithmetic and copies ran while one was open for 9% -> 17% of each run, Pallas kernels for 0% -> 77%
where the time goes in v1:
time: 436 us; the launch traced here: 431 us
  Pallas kernels  331 us (76%)
  local copies, waits for them, and re-layouts  73.1 us (17%)
  starting transfers between devices  15 us (3%)
  other arithmetic  7.18 us (2%)
    pallas_call x1, Pallas kernels, run_layer(): pl.pallas_call(functools.partial(layer_kernel, dims), out_shape=out_shape...  331 us
    reshape x3, local copies, waits for them, and re-layouts, per_device(): gu.astype(F32).reshape(blks, R, n, Fr).transpose(1, 2, 0, 3).reshape(R, FF)  19.3 us
    ppermute x7, starting transfers between devices, cond_rows_all(): moved = lax.ppermute(part, 'dp', perm) if step else part  15 us
    reshape x3, local copies, waits for them, and re-layouts, per_device(): gq[:, :, :3 * Q].astype(F32).reshape(blks, R, 3, Q).transpose(1, 2, 0, 3)  11 us
  transfers between devices with their start and end apart: 7, of which 0 were waited for; matrix products, arithmetic and copies ran while one was open for 17% of the time, Pallas kernels for 77%

profile of v1, /device:TPU:0, one launch (start us, length us, event | category | flops | bytes accessed | tf_op | source)
XLA Modules:
  0.0 430.7 jit_solution(3249042202761713649)
XLA Ops:
  0.8 0.9 reshape.206
  1.8 0.7 constant_dynamic-slice_fusion
  2.5 0.6 copy.86
  3.1 2.9 collective-permute-start
  6.0 0.6 copy.85
  6.6 1.6 collective-permute-start.1
  8.2 0.6 copy.84
  8.8 2.6 collective-permute-start.2
  11.3 0.6 copy.83
  11.9 1.2 collective-permute-start.3
  13.2 0.6 copy.82
  13.8 2.6 collective-permute-start.4
  16.4 0.7 fusion.5
  17.1 1.7 copy.51.refs_2_
  18.8 0.7 fusion.10
  19.5 0.8 copy.52.refs_4_
  20.4 0.7 copy.79
  21.1 0.6 reshape.196.refs_6_
  22.1 0.7 reshape.178.refs_7_
  22.7 0.6 reshape.197.refs_8_
  23.5 0.7 reshape.179.refs_9_
  24.2 0.6 reshape.199.refs_10_
  24.8 0.9 reshape.180
  25.7 2.3 dynamic-slice_reduce_fusion.1
  27.9 1.0 reshape.181.refs_12_
  28.9 0.4 reshape.182
  29.3 0.8 copy.78
  30.1 5.4 %reshape.183 = bf16[144,8,4,144]{3,2,1,0:T(4,128)(2,1)S(1)} reshape(bf16[144,4608]{1,0:T(8,128)(2,1)} %param.23) | data formatting | bytes 2654208 | tf_op jit(solution)/shard_map/reshape | solution.py:941
  35.5 3.8 dynamic-slice_reduce_fusion
  39.3 1.2 reshape.184.refs_14_
  40.5 1.7 constant_dynamic-slice_fusion.7.refs_15_
  42.2 331.2 %layer.1 = (bf16[256,1152]{1,0:T(8,128)(2,1)}, bf16[256,1152]{1,0:T(8,128)(2,1)}, f32[8,8,144]{2,1,0:T(8,128)}, bf16[4,8,16,768]{3,2,1,0:T(8,128)(2,1)}, bf16[4,...) custom-call(bf16[256,1152]{1,0:T(8,128)(2,1)} %bitcast.86, ...), custom_call_target="tpu_custom_call" | custom-call | tf_op jit(solution)/shard_map/layer/pallas_call | solution.py:881
  373.4 1.3 convert_reduce_fusion
  374.8 0.6 slice_reduce_fusion.1
  375.4 0.7 slice_reduce_fusion
  376.1 0.9 copy.53
  377.1 1.4 slice_convert_fusion
  378.7 0.6 fusion.12
  379.3 1.8 bitcast_convert_fusion
  381.4 0.3 copy.57
  381.7 0.4 copy-done.2
  382.2 0.7 copy-done.7
  382.9 0.8 convert_reduce_fusion.1
  383.6 0.6 copy.59
  384.3 4.1 reshape.211
  388.3 3.2 copy.54
  391.6 3.7 reshape.201
  395.3 4.1 collective-permute-start.5
  399.4 0.7 squeeze.52
  400.1 0.7 squeeze.53
  400.8 0.9 convert_element_type.87
  401.6 4.4 %reshape.213 = f32[4,144,8,144]{3,2,1,0:T(8,128)} reshape(bf16[4,144,1152]{2,1,0:T(8,128)(2,1)S(1)} %copy-done.4) | data formatting | bytes 3981312 | tf_op jit(solution)/shard_map/reshape | solution.py:984
  406.1 7.5 %copy.55 = f32[144,8,4,144]{3,2,1,0:T(4,128)} copy(f32[144,8,4,144]{3,1,0,2:T(8,128)} %bitcast.79) | data formatting | bytes 5308416 | tf_op jit(solution)/shard_map/reshape | solution.py:984
  413.6 7.3 %reshape.203 = f32[144,4608]{1,0:T(8,128)} reshape(f32[144,8,4,144]{3,2,1,0:T(4,128)} %copy.55) | data formatting | bytes 5308416 | tf_op jit(solution)/shard_map/reshape | solution.py:984
  421.0 0.7 reshape.192
  421.8 0.7 broadcast_in_dim.61
  422.6 0.7 broadcast_in_dim.62
  423.3 0.7 broadcast_in_dim.63
  424.0 0.7 broadcast_in_dim.64
  424.8 0.7 broadcast_in_dim.65
  425.7 2.7 convolution_bitcast_fusion
  428.4 0.8 copy.97
  429.2 0.5 copy-done.10
  429.7 0.8 copy.98
  (87 shorter events, 1.7 us)
Async XLA Ops:
  0.6 20.4 %copy-start.19 = (bf16[6912]{0:T(1024)(128)(2,1)S(1)}, bf16[6912]{0:T(1024)(128)(2,1)}, u32[]{:S(2)}) copy-start(bf16[6912]{0:T(1024)(128)(2,1)} %param.28) | copy-start | bytes 41476
  0.7 21.0 %copy-start.21 = (bf16[1152]{0:T(1024)(128)(2,1)S(1)}, bf16[1152]{0:T(1024)(128)(2,1)}, u32[]{:S(2)}) copy-start(bf16[1152]{0:T(1024)(128)(2,1)} %param.20) | copy-start | bytes 6916
  0.7 21.1 %copy-start.22 = (bf16[1152]{0:T(1024)(128)(2,1)S(1)}, bf16[1152]{0:T(1024)(128)(2,1)}, u32[]{:S(2)}) copy-start(bf16[1152]{0:T(1024)(128)(2,1)} %param.19) | copy-start | bytes 6916
  0.7 22.1 %copy-start.23 = (bf16[1152]{0:T(1024)(128)(2,1)S(1)}, bf16[1152]{0:T(1024)(128)(2,1)}, u32[]{:S(2)}) copy-start(bf16[1152]{0:T(1024)(128)(2,1)} %param.22) | copy-start | bytes 6916
  0.7 22.6 %copy-start.20 = (bf16[4608]{0:T(1024)(128)(2,1)S(1)}, bf16[4608]{0:T(1024)(128)(2,1)}, u32[]{:S(2)}) copy-start(bf16[4608]{0:T(1024)(128)(2,1)} %param.24) | copy-start | bytes 27652
  0.7 23.5 %copy-start.24 = (bf16[1152]{0:T(1024)(128)(2,1)S(1)}, bf16[1152]{0:T(1024)(128)(2,1)}, u32[]{:S(2)}) copy-start(bf16[1152]{0:T(1024)(128)(2,1)} %param.26) | copy-start | bytes 6916
  0.7 24.1 %copy-start.9 = (bf16[144,3456]{1,0:T(8,128)(2,1)S(1)}, bf16[144,3456]{1,0:T(8,128)(2,1)}, u32[]{:S(2)}) copy-start(bf16[144,3456]{1,0:T(8,128)(2,1)} %param.18) | copy-start | bytes 2985988
  3.1 392.2 %collective-permute-start = (bf16[7,144]{1,0:T(8,128)(2,1)}, bf16[7,144]{1,0:T(8,128)(2,1)}, u32[]{:S(2)}, u32[]{:S(2)}) collective-permute-start(bf16[7,144]{1,0:T(8,128)(2,1)} %bitcast.77), channel_id=1, source_target_pairs={{0,4},{4,8},{8,12},{12,16},{16,20},{20,24},{24,28},{28,0},{1,5},{5... | collective-permute-start | bytes 6056 | tf_op jit(solution)/shard_map/ppermute | solution.py:1001
  6.6 392.8 %collective-permute-start.1 = (bf16[7,144]{1,0:T(8,128)(2,1)}, bf16[7,144]{1,0:T(8,128)(2,1)}, u32[]{:S(2)}, u32[]{:S(2)}) collective-permute-start(bf16[7,144]{1,0:T(8,128)(2,1)} %bitcast.76), channel_id=1, source_target_pairs={{0,8},{4,12},{8,16},{12,20},{16,24},{20,28},{24,0},{28,4},{1,9},{5... | collective-permute-start | bytes 6056 | tf_op jit(solution)/shard_map/ppermute | solution.py:1001
  8.8 414.5 %collective-permute-start.2 = (bf16[7,144]{1,0:T(8,128)(2,1)}, bf16[7,144]{1,0:T(8,128)(2,1)}, u32[]{:S(2)}, u32[]{:S(2)}) collective-permute-start(bf16[7,144]{1,0:T(8,128)(2,1)} %bitcast.75), channel_id=1, source_target_pairs={{0,12},{4,16},{8,20},{12,24},{16,28},{20,0},{24,4},{28,8},{1,13},{... | collective-permute-start | bytes 6056 | tf_op jit(solution)/shard_map/ppermute | solution.py:1001
  11.9 412.1 %collective-permute-start.3 = (bf16[7,144]{1,0:T(8,128)(2,1)}, bf16[7,144]{1,0:T(8,128)(2,1)}, u32[]{:S(2)}, u32[]{:S(2)}) collective-permute-start(bf16[7,144]{1,0:T(8,128)(2,1)} %bitcast.74), channel_id=1, source_target_pairs={{0,16},{4,20},{8,24},{12,28},{16,0},{20,4},{24,8},{28,12},{1,17},{... | collective-permute-start | bytes 6056 | tf_op jit(solution)/shard_map/ppermute | solution.py:1001
  13.8 411.0 %collective-permute-start.4 = (bf16[7,144]{1,0:T(8,128)(2,1)}, bf16[7,144]{1,0:T(8,128)(2,1)}, u32[]{:S(2)}, u32[]{:S(2)}) collective-permute-start(bf16[7,144]{1,0:T(8,128)(2,1)} %bitcast.73), channel_id=1, source_target_pairs={{0,20},{4,24},{8,28},{12,0},{16,4},{20,8},{24,12},{28,16},{1,21},{... | collective-permute-start | bytes 6056 | tf_op jit(solution)/shard_map/ppermute | solution.py:1001
  24.8 4.1 copy-start.12
  42.2 334.8 %copy-start.14 = (bf16[1,7,1152]{2,1,0:T(8,128)(2,1)S(1)}, bf16[1,7,1152]{2,1,0:T(8,128)(2,1)}, u32[]{:S(2)}) copy-start(bf16[1,7,1152]{2,1,0:T(8,128)(2,1)} %param.16) | copy-start | bytes 48388
  373.4 3.7 copy-start.6
  377.1 1.5 copy-start.1
  377.1 2.2 copy-start.5
  379.3 1.8 copy-start
  381.4 0.8 copy-start.2
  382.2 0.7 copy-start.7
  391.6 3.7 copy-start.16
  391.6 7.8 %copy-start.18 = (f32[1,4,288]{2,1,0:T(4,128)S(1)}, f32[1,4,288]{2,1,0:T(4,128)}, u32[]{:S(2)}) copy-start(f32[1,4,288]{2,1,0:T(4,128)} %get-tuple-element.71) | copy-start | bytes 13828
  391.6 8.5 %copy-start.17 = (f32[1,4,288]{2,1,0:T(4,128)S(1)}, f32[1,4,288]{2,1,0:T(4,128)}, u32[]{:S(2)}) copy-start(f32[1,4,288]{2,1,0:T(4,128)} %get-tuple-element.70) | copy-start | bytes 13828
  391.6 9.2 %copy-start.13 = (bf16[144,1152]{1,0:T(8,128)(2,1)S(1)}, bf16[144,1152]{1,0:T(8,128)(2,1)}, u32[]{:S(2)}) copy-start(bf16[144,1152]{1,0:T(8,128)(2,1)} %get-tuple-element.28) | copy-start | bytes 995332
  391.6 10.1 %copy-start.4 = (bf16[4,144,1152]{2,1,0:T(8,128)(2,1)S(1)}, bf16[4,144,1152]{2,1,0:T(8,128)(2,1)}, u32[]{:S(2)}) copy-start(bf16[4,144,1152]{2,1,0:T(8,128)(2,1)} %get-tuple-element.30) | copy-start | bytes 3981316
  395.3 30.2 %collective-permute-start.5 = (bf16[7,144]{1,0:T(8,128)(2,1)S(1)}, bf16[7,144]{1,0:T(8,128)(2,1)S(1)}, u32[]{:S(2)}, u32[]{:S(2)}) collective-permute-start(bf16[7,144]{1,0:T(8,128)(2,1)S(1)} %bitcast.98), channel_id=1, source_target_pairs={{0,24},{4,28},{8,0},{12,4},{16,8},{20,12},{24,16},{28,20},{1,25},{... | collective-permute-start | bytes 6056 | tf_op jit(solution)/shard_map/ppermute | solution.py:1001
  399.4 26.2 %collective-permute-start.6 = (bf16[7,144]{1,0:T(8,128)(2,1)S(1)}, bf16[7,144]{1,0:T(8,128)(2,1)S(1)}, u32[]{:S(2)}, u32[]{:S(2)}) collective-permute-start(bf16[7,144]{1,0:T(8,128)(2,1)S(1)} %bitcast.97), channel_id=1, source_target_pairs={{0,28},{4,0},{8,4},{12,8},{16,12},{20,16},{24,20},{28,24},{1,29},{... | collective-permute-start | bytes 6056 | tf_op jit(solution)/shard_map/ppermute | solution.py:1001
  413.6 7.3 %copy-start.15 = (f32[4608]{0:T(1024)S(1)}, f32[4608]{0:T(1024)}, u32[]{:S(2)}) copy-start(f32[4608]{0:T(1024)} %slice_reduce_fusion) | copy-start | bytes 55300
  413.6 12.1 %copy-start.3 = (bf16[8,7,4608]{2,0,1:T(8,128)(2,1)S(1)}, bf16[8,7,4608]{2,0,1:T(8,128)(2,1)}, u32[]{:S(2)}) copy-start(bf16[8,7,4608]{2,0,1:T(8,128)(2,1)} %copy-done.2) | copy-start | bytes 1548292
  413.6 12.1 %copy-start.8 = (bf16[8,7,2304]{2,0,1:T(8,128)(2,1)S(1)}, bf16[8,7,2304]{2,0,1:T(8,128)(2,1)}, u32[]{:S(2)}) copy-start(bf16[8,7,2304]{2,0,1:T(8,128)(2,1)} %copy-done.7) | copy-start | bytes 774148
  425.7 2.7 copy-start.11
  428.4 1.3 copy-start.10

commit v2 on v1

v2 whole, which is shorter than its diff:
```python
import functools
import math

import jax
import jax.numpy as jnp
from jax import lax
from jax.experimental import pallas as pl
from jax.experimental.pallas import tpu as pltpu
from jax.sharding import PartitionSpec as P

HEADS = 16
BLKS = 4
BF = jnp.bfloat16
F32 = jnp.float32
MESH = pl.DeviceIdType.MESH
EPS = 1e-06


def up_to(value, multiple):
    return -(-value // multiple) * multiple


def nn(a, b):
    return lax.dot_general(a, b, (((1,), (0,)), ((), ())), preferred_element_type=F32)


def nt(a, b):
    return lax.dot_general(a, b, (((1,), (1,)), ((), ())), preferred_element_type=F32)


def tn(a, b):
    return lax.dot_general(a, b, (((0,), (0,)), ((), ())), preferred_element_type=F32)


def row_sums(values):
    return nn(jnp.ones((8, values.shape[0]), BF), values)[0:1]


def unit_rows(rows):
    centre = rows - jnp.mean(rows, axis=-1, keepdims=True)
    inverse = lax.rsqrt(jnp.mean(centre * centre, axis=-1, keepdims=True) + EPS)
    return centre * inverse, inverse


def norm_back(grad, normed, inverse):
    mean_grad = jnp.mean(grad, axis=-1, keepdims=True)
    mean_both = jnp.mean(grad * normed, axis=-1, keepdims=True)
    return inverse * (grad - mean_grad - normed * mean_both)


def layer_kernel(dims, *refs):
    T, D, n, sub, R, Q, HD, hpd, F, Fr, MODW = dims
    L, C3, WH, nz = BLKS * T, 3 * Q, D // 2, n // 2
    CP = up_to(C3, 128)
    MQ = up_to(-(-MODW // BLKS), 256)
    WE, WL = up_to(5 * D, 1024), up_to(2 * D + 4 * up_to(Q, 128), 1024)
    QE, QL = WE // 4, WL // 4
    QP = up_to(Q, 128)
    factor = HD ** (-0.5)
    (
        x_in, cot_in, lab_row, cond_in, query_b, value_b, out_bias, down_bias, up_bias, ad_bias,
        ad_h, wq_h, wo_h, wu_h, wd_h,
        out_o, gtok_o, cond_rx, dcond_o, ball_e, ball_l, gd_o, gu_o, gq_o, gw_o, na_h,
        wq, wo, wu, wd, ad, qkv_b, up_b, ad_b, cond_tx, pm_tx, pm_rx, mod4, mod3,
        na, dbm, act, gp, q3, lse, att_tx, att_rx, datt_tx, mid, dmid, bra,
        ps, rs_a, rs_b, gd, gu, gw, gd_x, gu_x, gq_x, gw_x, gw_z,
        fin_w, dk_acc, dv_acc, sb_e, sb_l, btx_e, btx_l, brx_e, brx_l, dc_tx,
        loc, g_s, g_r, o_s, o_r, c_s, c_r, p_s, p_r, m_s, m_r, ag_s, ag_r, a_s, a_r, r_s, r_r,
        x_s, x_r, f_s, f_r, b1_s, b1_r, b2_s, b2_r, b3_s, b3_r, d_s, d_r, w_s, w_r,
    ) = refs

    dp = lax.axis_index("dp")
    b = lax.axis_index("blk")
    g, member = dp // sub, dp % sub
    zi, xi = g // 2, g % 2
    core = b % 2
    b1, b2, b3 = b + 1 - 2 * core, (b + 2) % 4, 3 - b

    def rel(k):
        return ((b // 2 + k // 2) % 2) * 2 + (b % 2 + k % 2) % 2

    def at_dp(group):
        return (group * sub + member, b)

    def at_blk(index):
        return (dp, index)

    gx = g + 1 - 2 * xi

    place = zi + xi * (n - 1 - 2 * zi)
    first_rows = up_to(R // 2, 16)

    def group_at(position):
        position = (position + 2 * n) % n
        back = position // nz
        return 2 * (position + back * (n - 1 - 2 * position)) + back

    def remote(src, dst, ssem, rsem, where):
        return pltpu.make_async_remote_copy(
            src_ref=src, dst_ref=dst, send_sem=ssem, recv_sem=rsem, device_id=where, device_id_type=MESH
        )

    def strip(i):
        return pl.ds(pl.multiple_of(T * i, T), T)

    def rows_of(i, size):
        return pl.ds(pl.multiple_of(size * i, size), size)

    FF = BLKS * F
    stage_cp = [
        pltpu.make_async_copy(src.at[:, pl.ds(D * p, D)], gd.at[pl.ds(R * to, R), :], loc.at[10 + to])
        for to, (src, p) in enumerate(
            [(wq_h, 0), (wq_h, 1), (wq_h, 2), (wo_h, 0), (wu_h, 0), (wu_h, 1), (wu_h, 2), (wu_h, 3)]
        )
    ]
    for cp in stage_cp:
        cp.start()
    own_d = pltpu.make_async_copy(wd_h.at[rows_of(b, Fr), :], wd.at[rows_of(g, Fr), :], loc.at[3])
    own_d.start()

    def flat(ref):
        return ref[...].astype(F32).reshape(1, -1)

    ad_b[...] = flat(ad_bias)

    barrier = pltpu.get_barrier_semaphore()
    for k in range(1, n):
        pl.semaphore_signal(barrier, inc=1, device_id=at_dp((g + k) % n), device_id_type=MESH)
    for other in (b1, b2, b3):
        pl.semaphore_signal(barrier, inc=1, device_id=at_blk(other), device_id_type=MESH)
    pl.semaphore_wait(barrier, n - 1 + 3)

    cond = cond_in[...].astype(F32)
    cond = (cond / (1.0 + jnp.exp(-cond))).astype(BF).astype(F32)
    cond = jnp.concatenate([cond, jnp.zeros((8 - cond.shape[0], D), F32)], axis=0)
    for gg in range(n):
        cond_tx[gg] = cond[:, R * gg : R * (gg + 1)]
    cond_rx[g] = cond_tx[g]
    cond_cp = [
        remote(cond_tx.at[(g + k) % n], cond_rx.at[g], c_s.at[k], c_r.at[k], at_dp((g + k) % n))
        for k in range(1, n)
    ]
    for cp in cond_cp:
        cp.start()

    def piece(size, i, half):
        first = first_rows if half else 0
        return pl.ds(pl.multiple_of(size * i + first, 16), size - first_rows if half else first_rows)

    class Gather:
        def __init__(self, slot, ref):
            self.copies = {}
            for way in range(2):
                sign = 1 - 2 * way
                for half in range(2):
                    for step in range(nz if half == way else nz - 1):
                        at = ref.at[piece(R, group_at(place - sign * step), half), :]
                        flow = 2 * way + half
                        self.copies[way, half, step] = remote(
                            at, at, g_s.at[slot, flow, step], g_r.at[slot, flow, step], at_dp(group_at(place + sign))
                        )

        def start(self):
            for half in range(2):
                for way in range(2):
                    self.copies[way, half, 0].start()

        def hop(self, step):
            for half in range(2):
                for way in range(2):
                    self.copies[way, half, step - 1].wait_recv()
                    if (way, half, step) in self.copies:
                        self.copies[way, half, step].start()

        def arrive(self):
            for way in range(2):
                self.copies[way, way, nz - 1].wait_recv()

        def done(self):
            for copy in self.copies.values():
                copy.wait_send()

    take_q, take_o = Gather(0, wq), Gather(1, wo.at[core])
    take_u, take_d = Gather(2, wu), Gather(3, wd)
    for cp in stage_cp[:3]:
        cp.wait()
    for j in range(BLKS):

        @pl.when(b == j)
        def _():
            own = [gd[R * p : R * (p + 1), Q * j : Q * (j + 1)] for p in range(3)]
            wq[rows_of(g, R), :] = jnp.concatenate(own, axis=1)

    take_q.start()
    start = pl.multiple_of(jnp.minimum(MQ * b, MODW - MQ), 128)
    ad_cp = pltpu.make_async_copy(ad_h.at[:, pl.ds(start, MQ)], ad, loc.at[4])
    ad_cp.start()

    for cp in cond_cp:
        cp.wait_recv()
    ad_cp.wait()
    cond_all = cond_rx[...].reshape(n * 8, R).astype(BF)
    partial = nn(cond_all, ad[...]).reshape(n, 8, MQ)
    halves = jnp.concatenate([partial[:, :, : MQ // 2], partial[:, :, MQ // 2 :]], axis=1)
    pm_tx[...] = halves.astype(BF)
    pm_rx[g] = pm_tx[g]
    part_cp = [
        remote(pm_tx.at[(g + k) % n], pm_rx.at[g], p_s.at[k], p_r.at[k], at_dp((g + k) % n))
        for k in range(1, n)
    ]
    for cp in part_cp:
        cp.start()
    for cp in stage_cp[3:]:
        cp.wait()
    for j in range(BLKS):

        @pl.when(b == j)
        def _():
            own = [
                gd[R * (4 + (p // D)) : R * (5 + (p // D)), p % D : p % D + Fr]
                for p in range(Fr * j, FF, BLKS * Fr)
            ]
            wu[rows_of(g, R), :] = jnp.concatenate(own, axis=1)
            at = slice(Q * j, Q * (j + 1))
            parts = [flat(query_b)[:, at], jnp.zeros((1, Q), F32), flat(value_b)[:, at]]
            qkv_b[...] = jnp.concatenate(parts, axis=1)
            every = flat(up_bias)
            own = [every[:, p : p + Fr] for p in range(Fr * j, FF, BLKS * Fr)]
            up_b[...] = jnp.concatenate(own, axis=1)

    for j in range(2):

        @pl.when(core == j)
        def _():
            wo[j, rows_of(g, R), :] = gd[3 * R : 4 * R, WH * j : WH * (j + 1)]

    one_hot = lab_row[...] == lax.broadcasted_iota(jnp.int32, (8, L), 0)
    column = lax.broadcasted_iota(jnp.int32, (8, 128), 0).astype(BF)
    labels = tn(one_hot.astype(BF), column)
    lse[:, hpd : hpd + 1] = labels[:, 0:1]
    row_labels = lab_row[...].astype(F32)
    take_q.hop(1)
    for cp in part_cp:
        cp.wait_recv()
    total = jnp.sum(pm_rx[...].astype(F32), axis=0)
    own_mod = jnp.concatenate([total[:8], total[8:]], axis=1) + ad_b[:, pl.ds(start, MQ)]
    mod4[b] = own_mod
    mod_cp = [
        remote(mod4.at[b], mod4.at[b], m_s.at[k], m_r.at[k], at_blk(rel(k))) for k in range(1, 4)
    ]
    for cp in mod_cp:
        cp.start()
    for cp in mod_cp:
        cp.wait_recv()
    for j in range(BLKS):
        first = min(MQ * j, MODW - MQ)
        skip = MQ * j - first
        value = mod4[j][:, skip:]
        high = value.astype(BF).astype(F32)
        middle = (value - high).astype(BF).astype(F32)
        parts = jnp.concatenate([high, middle, value - high - middle], axis=0)
        mod3[:, MQ * j : min(MQ * (j + 1), MODW)] = parts.astype(BF)
    CH = T // 2

    def by_chunk(step):
        def body(c, carry):
            step(pl.ds(pl.multiple_of(CH * c, CH), CH), pl.ds(pl.multiple_of(T * b + CH * c, CH), CH))
            return carry

        lax.fori_loop(0, T // CH, body, 0)

    def crop_of(rows, width):
        crops = jnp.bitwise_and(lax.broadcasted_iota(jnp.int32, (CH, width), 1), 7).astype(F32)
        return (lse[rows, hpd : hpd + 1] == crops).astype(BF)

    def per_token(chooser, piece):
        return nn(chooser, mod3[:, D * piece : D * (piece + 1)])

    def per_crop(chooser, values):
        high = values.astype(BF)
        return tn(chooser, high) + tn(chooser, (values - high.astype(F32)).astype(BF))

    class Spread:
        def __init__(self, slot, buffer):
            def copy(index, src, where):
                return remote(
                    buffer.at[strip(src), :], buffer.at[strip(src), :], ag_s.at[slot, index], ag_r.at[slot, index],
                    at_blk(where),
                )

            self.near = copy(0, b, b1)
            self.far = copy(1, b, b2)
            self.onward = copy(2, b2, b1)

        def start(self):
            self.far.start()
            self.near.start()

        def forward(self):
            self.far.wait_recv()
            self.onward.start()

        def done(self):
            self.near.wait_send()
            self.far.wait_send()
            self.onward.wait_send()

    def begin(at, rows):
        normed, _ = unit_rows(x_in[at, :].astype(F32))
        chooser = crop_of(rows, 24)
        na[rows, :] = (normed * (1.0 + per_token(chooser, 1)) + per_token(chooser, 0)).astype(BF)

    by_chunk(begin)
    spread_a = Spread(0, na)
    spread_a.start()

    def begin_back(at, rows):
        dbm[rows, :] = (per_token(crop_of(rows, 24), 5) * cot_in[at, :].astype(F32)).astype(BF)

    by_chunk(begin_back)
    sb_e[...] = jnp.zeros_like(sb_e)
    sb_l[...] = jnp.zeros_like(sb_l)
    sb_e[1:2, 4 * D : 5 * D] = row_sums(dbm[strip(b), :])
    take_q.hop(2)
    take_q.hop(3)
    take_o.start()
    take_q.arrive()

    def project(k):
        i = rel(k)
        packed = nn(na[strip(i), :], wq[...]) + qkv_b[...]
        for s in range(3 * hpd):
            q3[s, strip(i), :] = packed[:, HD * s : HD * (s + 1)].astype(BF)

    def project_loop(lo, hi):
        def body(k, carry):
            project(k)
            return carry

        lax.fori_loop(lo, hi, body, 0)

    project_loop(0, 1)
    spread_a.near.wait_recv()
    project_loop(1, 2)
    spread_a.forward()
    project_loop(2, 3)
    take_o.hop(1)
    spread_a.onward.wait_recv()
    project_loop(3, 4)
    keep_na = pltpu.make_async_copy(na, na_h, loc.at[5])
    keep_na.start()
    spread_d = Spread(1, dbm)
    spread_d.start()
    own_d.wait()

    def attend(i):
        mask = lse[strip(i), hpd : hpd + 1] == row_labels
        pieces, logs = [], []
        for h in range(hpd):
            scores = nt(q3[h, strip(i), :], q3[hpd + h]) * factor
            scores = jnp.where(mask, scores, -1e30)
            top = jnp.max(scores, axis=-1, keepdims=True)
            raised = jnp.exp(scores - top)
            sums = jnp.sum(raised, axis=-1, keepdims=True)
            pieces.append(nn(raised.astype(BF), q3[2 * hpd + h]) / sums)
            logs.append(top + jnp.log(sums))
        att_tx[i] = jnp.concatenate(pieces, axis=1).astype(BF)
        lse[strip(i), 0:hpd] = jnp.concatenate(logs, axis=1)

    att_cp = {
        k: remote(att_tx.at[rel(k)], att_rx.at[b], a_s.at[0, k], a_r.at[0, k], at_blk(rel(k)))
        for k in range(1, 4)
    }
    for turn, k in enumerate((2, 3, 1, 0)):
        attend(rel(k))
        if turn == 0:
            keep_na.wait()
            spread_a.done()
        if k:
            att_cp[k].start()
        if turn == 0:
            take_o.hop(2)
        if turn == 1:
            take_o.hop(3)
            take_u.start()
        if turn == 2:
            take_o.arrive()
            share_o = remote(wo.at[core], wo.at[core], o_s.at[0], o_r.at[0], at_blk(b1))
            share_o.start()
        if turn == 3:
            spread_d.forward()
    att_rx[b] = att_tx[b]
    for k in range(1, 4):
        att_cp[k].wait_recv()
    share_o.wait_recv()
    attf = jnp.concatenate([att_rx[j] for j in range(BLKS)], axis=1)
    branch_a = jnp.concatenate([nn(attf, wo[0]), nn(attf, wo[1])], axis=1) + flat(out_bias)
    bra[...] = branch_a

    def between(at, rows):
        chooser = crop_of(rows, 24)
        middle = x_in[at, :].astype(F32) + per_token(chooser, 2) * bra[at, :]
        mid[at, :] = middle
        normed, _ = unit_rows(middle)
        na[rows, :] = (normed * (1.0 + per_token(chooser, 4)) + per_token(chooser, 3)).astype(BF)

    by_chunk(between)
    spread_m = Spread(2, na)
    spread_m.start()

    c0, c1 = math.sqrt(2.0 / math.pi), 0.044715

    def feed(k):
        i = rel(k)
        hidden = nn(na[strip(i), :], wu[...]) + up_b[...]
        square = hidden * hidden
        bent = jnp.tanh(c0 * (hidden + c1 * hidden * square))
        half = 0.5 * (1.0 + bent)
        act[strip(i), :] = (hidden * half).astype(BF)
        slope = half + 0.5 * hidden * (1.0 - bent * bent) * (c0 * (1.0 + (3.0 * c1) * square))
        gp[strip(i), :] = slope.astype(BF)

    def feed_down(k):
        i = rel(k)
        na[strip(i), :] = nn(act[strip(i), :], wd[...]).astype(BF)

    def loop(lo, hi, step):
        def body(k, carry):
            step(k)
            return carry

        lax.fori_loop(lo, hi, body, 0)

    class Reduce:
        def __init__(self, slot, buffer, rx):
            self.buffer, self.rx = buffer, rx

            def copy(index, src, where):
                return remote(
                    buffer.at[strip(src), :], rx.at[index], r_s.at[slot, index], r_r.at[slot, index], at_blk(where)
                )

            self.near, self.pair, self.far = copy(0, b1, b1), copy(1, b3, b1), copy(2, b2, b2)

        def cross(self):
            self.pair.wait_recv()
            total = self.buffer[strip(b2), :].astype(F32) + self.rx[1].astype(F32)
            self.buffer[strip(b2), :] = total.astype(BF)
            self.far.start()

        def arrive(self):
            self.near.wait_recv()
            self.far.wait_recv()
            self.near.wait_send()
            self.pair.wait_send()
            self.far.wait_send()

        def result(self, at, rows):
            total = self.buffer[rows, :].astype(F32) + self.rx[0, at, :].astype(F32)
            return total + self.rx[2, at, :].astype(F32)

    take_u.hop(1)
    spread_m.near.wait_recv()
    take_u.hop(2)
    spread_m.forward()
    take_u.hop(3)
    take_d.start()
    spread_m.onward.wait_recv()
    take_u.arrive()
    loop(0, 4, feed)

    spread_d.near.wait_recv()
    spread_d.onward.wait_recv()

    class Scatter:
        def __init__(self, slot, grad, rx, dest):
            self.grad, self.rx, self.dest, self.cols = grad, rx, dest, rx.shape[3]
            self.copies = {}
            for way in range(2):
                sign = 1 - 2 * way
                for half in range(2):
                    far = nz if half == way else nz - 1
                    for left in range(far):
                        where = piece(R, 0, half)
                        if left == far - 1:
                            owner = group_at(place + sign * far)
                            src = grad.at[piece(R, owner, half), pl.ds(0, self.cols)]
                        else:
                            src = rx.at[way, left + 1, where, :]
                        flow = 2 * way + half
                        self.copies[way, half, left] = remote(
                            src, rx.at[way, left, where, :], x_s.at[slot, flow, left], x_r.at[slot, flow, left],
                            at_dp(group_at(place + sign)),
                        )
            own = rx.at[0, 0]
            self.local = pltpu.make_async_copy(own, dest.at[b], loc.at[6 + slot])
            self.near = remote(own, dest.at[b], f_s.at[slot, 0], f_r.at[slot, 0], at_blk(b1))
            self.far = remote(own, dest.at[b], f_s.at[slot, 1], f_r.at[slot, 1], at_blk(b2))
            self.onward = remote(dest.at[b2], dest.at[b2], f_s.at[slot, 2], f_r.at[slot, 2], at_blk(b1))

        def start(self):
            for way in range(2):
                self.copies[way, way, nz - 1].start()
            for way in range(2):
                self.copies[way, 1 - way, nz - 2].start()

        def pump(self, left):
            for other in (1, 0):
                for way in range(2):
                    half = 1 - way if other else way
                    if left == nz - 1 and other:
                        continue
                    self.copies[way, half, left].wait_recv()
                    owner = group_at(place + (1 - 2 * way) * left)
                    first = first_rows if half else 0
                    last = R if half else first_rows
                    own = self.grad[piece(R, owner, half), 0 : self.cols].astype(F32)
                    total = own + self.rx[way, left, first:last, :].astype(F32)
                    self.rx[way, left, first:last, :] = total.astype(BF)
                    self.copies[way, half, left - 1].start()

        def total(self):
            for way in range(2):
                for half in range(2):
                    self.copies[way, half, 0].wait_recv()
            own = self.grad[rows_of(g, R), 0 : self.cols].astype(F32)
            own = own + self.rx[0, 0].astype(F32) + self.rx[1, 0].astype(F32)
            self.rx[0, 0] = own.astype(BF)
            self.far.start()
            self.near.start()
            self.local.start()

        def forward(self):
            self.far.wait_recv()
            self.onward.start()

        def done(self):
            self.near.wait_recv()
            self.onward.wait_recv()
            self.local.wait()
            self.near.wait_send()
            self.far.wait_send()
            self.onward.wait_send()
            for copy in self.copies.values():
                copy.wait_send()

    give_d = Scatter(0, gd, gd_x, gd_o)
    give_u = Scatter(1, gu, gu_x, gu_o)
    give_q = Scatter(2, wu, gq_x, gq_o)

    def hidden_back(k):
        i = rel(k)
        d_active = nt(dbm[strip(i), :], wd[...])
        gp[strip(i), :] = (gp[strip(i), :].astype(F32) * d_active).astype(BF)

    def tiles(size):
        return 384 if size % 384 == 0 else size

    def weight_grad(dest, left, right, size):
        step = tiles(size)

        def body(j, carry):
            at = pl.ds(pl.multiple_of(step * j, step), step)
            dest[at, :] = tn(left[:, at], right[...]).astype(BF)
            return carry

        lax.fori_loop(0, size // step, body, 0)

    take_d.hop(1)
    weight_grad(gd, act, dbm, F)
    give_d.start()
    take_d.hop(2)
    take_d.hop(3)
    take_d.arrive()
    loop(0, 4, hidden_back)
    give_d.pump(3)
    at_e7 = pl.ds(pl.multiple_of(F * b, 128), F)

    def up_back(k):
        i = rel(k)
        ps[strip(i), :] = nt(gp[strip(i), :], wu[...]).astype(BF)

    spread_d.done()
    reduce_m = Reduce(1, ps, rs_b)
    loop(3, 4, up_back)
    reduce_m.pair.start()
    loop(2, 3, up_back)
    reduce_m.cross()
    loop(1, 2, up_back)
    reduce_m.near.start()
    loop(0, 1, up_back)
    weight_grad(gu, na, gp, D)
    give_u.start()
    give_d.pump(2)
    spread_m.done()
    reduce_f = Reduce(0, na, rs_a)
    loop(3, 4, feed_down)
    reduce_f.pair.start()
    loop(1, 3, feed_down)
    reduce_f.near.start()
    loop(0, 1, feed_down)
    up_sums = row_sums(gp[...])
    give_d.pump(1)
    reduce_m.arrive()

    def middle_back(at, rows):
        d_normed = reduce_m.result(at, rows)
        ps[rows, :] = d_normed.astype(BF)
        normed, inverse = unit_rows(mid[at, :])
        chooser = crop_of(rows, 24)
        d_normed = d_normed * (1.0 + per_token(chooser, 4))
        d_middle = cot_in[at, :].astype(F32) + norm_back(d_normed, normed, inverse)
        dmid[at, :] = d_middle
        dbm[rows, :] = (per_token(chooser, 2) * d_middle).astype(BF)

    by_chunk(middle_back)

    own_rows = dbm[strip(b), :]
    d_att = (nt(own_rows[:, :WH], wo[0]) + nt(own_rows[:, WH:], wo[1])).astype(BF)
    for j in range(BLKS):
        datt_tx[j] = d_att[:, Q * j : Q * (j + 1)]
    datt_cp = {
        k: remote(datt_tx.at[rel(k)], att_rx.at[b], a_s.at[1, k], a_r.at[1, k], at_blk(rel(k)))
        for k in range(1, 4)
    }
    for k in (2, 3, 1):
        datt_cp[k].start()
    spread_w = Spread(3, dbm)
    spread_w.start()
    give_u.pump(3)
    give_d.total()
    reduce_f.cross()
    att_rx[b] = datt_tx[b]

    def middle_sums(at, rows):
        chooser = crop_of(rows, 8)
        normed, _ = unit_rows(mid[at, :])
        d_normed = ps[rows, :].astype(F32)
        sb_e[:, 0:D] += per_crop(chooser, dmid[at, :] * bra[at, :])
        sb_e[:, D : 2 * D] += per_crop(chooser, d_normed)
        sb_e[:, 2 * D : 3 * D] += per_crop(chooser, d_normed * normed)

    by_chunk(middle_sums)
    sb_e[0:1, 4 * D : 5 * D] = row_sums(dbm[strip(b), :])

    class Bundle:
        def __init__(self, slot, sums, tx, rx, ball, quarter):
            self.sums, self.tx, self.rx, self.ball, self.quarter = sums, tx, rx, ball, quarter
            self.one = [
                remote(tx.at[rel(k)], rx.at[b], b1_s.at[slot, k], b1_r.at[slot, k], at_blk(rel(k)))
                for k in range(1, 4)
            ]
            self.two = [
                remote(ball.at[b, g], ball.at[b, g], b2_s.at[slot, k], b2_r.at[slot, k], at_dp((g + k) % n))
                for k in range(1, n)
            ]
            self.three = [
                remote(ball.at[b], ball.at[b], b3_s.at[slot, k], b3_r.at[slot, k], at_blk(rel(k)))
                for k in range(1, 4)
            ]

        def start(self):
            half = self.quarter // 2
            for j in range(BLKS):
                first = self.sums[:, 2 * half * j : 2 * half * j + half]
                second = self.sums[:, 2 * half * j + half : 2 * half * (j + 1)]
                self.tx[j] = jnp.concatenate([first, second], axis=0).astype(BF)
            self.rx[b] = self.tx[b]
            for cp in self.one:
                cp.start()

        def groups(self):
            for cp in self.one:
                cp.wait_recv()
            self.ball[b, g] = jnp.sum(self.rx[...].astype(F32), axis=0).astype(BF)
            for cp in self.two:
                cp.start()

        def share(self):
            for cp in self.two:
                cp.wait_recv()
            for cp in self.three:
                cp.start()

        def arrive(self):
            for cp in self.three:
                cp.wait_recv()

        def done(self):
            for cp in self.one + self.two + self.three:
                cp.wait_send()

    bundle_e = Bundle(0, sb_e, btx_e, brx_e, ball_e, QE)
    bundle_l = Bundle(1, sb_l, btx_l, brx_l, ball_l, QL)
    for k in range(1, 4):
        datt_cp[k].wait_recv()

    def head_back(h):
        dk_acc[...] = jnp.zeros_like(dk_acc)
        dv_acc[...] = jnp.zeros_like(dv_acc)

        def body(i, carry):
            at = strip(i)
            query, keys, values = q3[h, at, :], q3[hpd + h], q3[2 * hpd + h]
            mask = lse[at, hpd : hpd + 1] == row_labels
            scores = jnp.where(mask, nt(query, keys) * factor, -1e30)
            probs = jnp.exp(scores - lse[at, h : h + 1])
            d_out = att_rx[i, :, HD * h : HD * (h + 1)]
            kept = att_tx[i, :, HD * h : HD * (h + 1)]
            delta = jnp.sum(d_out.astype(F32) * kept.astype(F32), axis=-1, keepdims=True)
            dv_acc[...] += tn(probs.astype(BF), d_out)
            d_scores = (probs * (nt(d_out, values) - delta)).astype(BF)
            dk_acc[...] += tn(d_scores, query)
            q3[h, at, :] = (nn(d_scores, keys) * factor).astype(BF)
            return carry

        lax.fori_loop(0, BLKS, body, 0)
        q3[hpd + h] = (dk_acc[...] * factor).astype(BF)
        q3[2 * hpd + h] = dv_acc[...].astype(BF)

    class OutScatter:
        def __init__(self):
            self.x = remote(gw.at[rows_of(1 - xi, R), :], gw_x, w_s.at[0], w_r.at[0], at_dp(gx))
            at = jnp.maximum((zi - b + nz) % nz, 1) - 1
            self.z = remote(gw_x, gw_z.at[at], w_s.at[1], w_r.at[1 + at], at_dp(2 * b + xi))
            self.local = pltpu.make_async_copy(fin_w, gw_o, loc.at[9])
            self.out = [
                remote(fin_w, gw_o, w_s.at[1 + k], w_r.at[nz + 1], at_blk(rel(k))) for k in range(1, 4)
            ]

        def start(self):
            self.x.start()

        def cross(self):
            self.x.wait_recv()
            total = gw[rows_of(xi, R), :].astype(F32) + gw_x[...].astype(F32)
            gw_x[...] = total.astype(BF)

            @pl.when(zi != b)
            def _():
                self.z.start()

        def total(self):
            @pl.when(zi == b)
            def _():
                own = gw_x[...].astype(F32)
                for k in range(1, nz):
                    remote(gw_x, gw_z.at[k - 1], w_s.at[0], w_r.at[k], at_dp(gx)).wait_recv()
                    own = own + gw_z[k - 1].astype(F32)
                fin_w[...] = own.astype(BF)
                for cp in self.out:
                    cp.start()
                self.local.start()

        def done(self):
            self.x.wait_send()

            @pl.when(zi != b)
            def _():
                self.z.wait_send()
                self.out[0].wait_recv()

            @pl.when(zi == b)
            def _():
                for cp in self.out:
                    cp.wait_send()
                self.local.wait()

    take_d.done()
    pieces_cp = [
        pltpu.make_async_copy(ad_h.at[:, pl.ds(D * p, D)], wd.at[pl.ds(R * p, R), pl.ds(0, D)], loc.at[10 + p])
        for p in range(6)
    ]
    for cp in pieces_cp:
        cp.start()
    give_w = OutScatter()
    head_back(0)
    give_u.pump(2)
    spread_w.forward()
    head_back(1)
    give_u.pump(1)
    give_d.forward()
    spread_w.near.wait_recv()
    spread_w.onward.wait_recv()
    att_all = att_tx[...].reshape(L, Q)
    gw[...] = tn(att_all, dbm[...]).astype(BF)
    give_w.start()
    head_back(2)
    reduce_f.arrive()

    def end(at, rows):
        branch_m = reduce_f.result(at, rows) + flat(down_bias)
        out_o[at, :] = (mid[at, :] + per_token(crop_of(rows, 24), 5) * branch_m).astype(BF)
        sb_e[:, 3 * D : 4 * D] += per_crop(crop_of(rows, 8), cot_in[at, :].astype(F32) * branch_m)

    by_chunk(end)
    na_back = pltpu.make_async_copy(na_h, na, loc.at[5])
    na_back.start()
    sb_e[7:8, at_e7] = up_sums
    bundle_e.start()
    give_w.cross()
    head_back(3)
    give_u.total()
    bundle_e.groups()

    def back_rows(i):
        return jnp.concatenate([q3[s, strip(i), :] for s in range(3 * hpd)], axis=1)

    def qkv_back(k):
        i = rel(k)
        d_packed = back_rows(i)
        act[strip(i), 0:C3] = d_packed
        ps[strip(i), :] = nt(d_packed, wq[...]).astype(BF)

    reduce_a = Reduce(2, ps, rs_a)
    loop(3, 4, qkv_back)
    reduce_a.pair.start()
    loop(2, 3, qkv_back)
    reduce_a.cross()
    loop(1, 2, qkv_back)
    reduce_a.near.start()
    loop(0, 1, qkv_back)
    na_back.wait()
    take_u.done()
    step = tiles(D)

    def grad_body(j, carry):
        at = pl.ds(pl.multiple_of(step * j, step), step)
        wu[at, 0:C3] = tn(na[:, at], act[:, 0:C3]).astype(BF)
        return carry

    lax.fori_loop(0, D // step, grad_body, 0)
    give_q.start()
    give_u.forward()
    give_w.total()
    bundle_e.share()
    bias_sums = row_sums(act[:, 0:C3])
    pad = jnp.zeros((1, QP - Q), F32)
    at_l = pl.ds(pl.multiple_of(2 * D + QP * b, 128), QP)
    sb_l[0:1, at_l] = jnp.concatenate([bias_sums[:, :Q], pad], axis=1)
    sb_l[1:2, at_l] = jnp.concatenate([bias_sums[:, 2 * Q :], pad], axis=1)
    reduce_a.arrive()

    def token_sums(at, rows):
        chooser = crop_of(rows, 8)
        normed, _ = unit_rows(x_in[at, :].astype(F32))
        d_normed = reduce_a.result(at, rows)
        sb_l[:, 0:D] += per_crop(chooser, d_normed)
        sb_l[:, D : 2 * D] += per_crop(chooser, d_normed * normed)

    by_chunk(token_sums)
    give_q.pump(3)
    bundle_l.start()

    def token_back(at, rows):
        normed, inverse = unit_rows(x_in[at, :].astype(F32))
        d_normed = reduce_a.result(at, rows) * (1.0 + per_token(crop_of(rows, 24), 1))
        gtok_o[at, :] = (dmid[at, :] + norm_back(d_normed, normed, inverse)).astype(BF)

    by_chunk(token_back)
    bundle_l.groups()
    give_q.pump(2)
    bundle_e.arrive()
    for cp in pieces_cp:
        cp.wait()

    def crop_part(ball, j, columns, half, first, width):
        both = ball[j].astype(F32)
        rows = both[:, 0:8, :] if half == 0 else both[:, 8:16, :]
        rows = rows.reshape(n * 8, columns).astype(BF)
        total, at = 0.0, first
        while at < first + width:
            p = at // D
            end = min(first + width, D * (p + 1))
            total = total + nt(rows[:, at - first : end - first], wd[R * p : R * (p + 1), at - D * p : end - D * p])
            at = end
        return total

    d_cond = jnp.zeros((n * 8, R), F32)
    for j in range(BLKS):
        for half in range(2):
            first = QE * j + half * (QE // 2)
            width = min(QE // 2, 4 * D - first)
            if width > 0:
                d_cond = d_cond + crop_part(ball_e, j, QE // 2, half, 2 * D + first, width)
    bundle_l.share()
    give_q.pump(1)
    bundle_l.arrive()
    for j in range(BLKS):
        for half in range(2):
            first = QL * j + half * (QL // 2)
            width = min(QL // 2, 2 * D - first)
            if width > 0:
                d_cond = d_cond + crop_part(ball_l, j, QL // 2, half, first, width)
    dc_tx[...] = d_cond.reshape(n, 8, R)
    dcond_o[g] = dc_tx[g]
    dcond_cp = [
        remote(dc_tx.at[(g + k) % n], dcond_o.at[g], d_s.at[k], d_r.at[k], at_dp((g + k) % n))
        for k in range(1, n)
    ]
    for cp in dcond_cp:
        cp.start()
    give_q.total()
    give_q.forward()
    for cp in dcond_cp:
        cp.wait_recv()

    give_q.done()
    give_d.done()
    give_u.done()
    give_w.done()
    bundle_e.done()
    bundle_l.done()
    for cp in cond_cp + part_cp + mod_cp + dcond_cp:
        cp.wait_send()
    for k in range(1, 4):
        att_cp[k].wait_send()
        datt_cp[k].wait_send()
    spread_w.done()
    share_o.wait_send()
    for take in (take_q, take_o):
        take.done()


def run_layer(dims, inputs):
    T, D, n, sub, R, Q, HD, hpd, F, Fr, MODW = dims
    L, C3, WH, nz = BLKS * T, 3 * Q, D // 2, n // 2
    CP = up_to(C3, 128)
    MQ = up_to(-(-MODW // BLKS), 256)
    WE, WL = up_to(5 * D, 1024), up_to(2 * D + 4 * up_to(Q, 128), 1024)
    vm = pl.BlockSpec(memory_space=pltpu.VMEM)
    hbm = pl.BlockSpec(memory_space=pl.ANY)
    out_shape = (
        jax.ShapeDtypeStruct((T, D), BF),
        jax.ShapeDtypeStruct((T, D), BF),
        jax.ShapeDtypeStruct((n, 8, R), F32),
        jax.ShapeDtypeStruct((n, 8, R), F32),
        jax.ShapeDtypeStruct((BLKS, n, 16, WE // 8), BF),
        jax.ShapeDtypeStruct((BLKS, n, 16, WL // 8), BF),
        jax.ShapeDtypeStruct((BLKS, Fr, D), BF),
        jax.ShapeDtypeStruct((BLKS, R, F), BF),
        jax.ShapeDtypeStruct((BLKS, R, CP), BF),
        jax.ShapeDtypeStruct((R, D), BF),
        jax.ShapeDtypeStruct((L, D), BF),
    )
    dma = pltpu.SemaphoreType.DMA
    scratch = [
        pltpu.VMEM((D, C3), BF),
        pltpu.VMEM((2, D, WH), BF),
        pltpu.VMEM((D, F), BF),
        pltpu.VMEM((F, D), BF),
        pltpu.VMEM((R, MQ), BF),
        pltpu.VMEM((1, C3), F32),
        pltpu.VMEM((1, F), F32),
        pltpu.VMEM((1, MODW), F32),
        pltpu.VMEM((n, 8, R), F32),
        pltpu.VMEM((n, 16, MQ // 2), BF),
        pltpu.VMEM((n, 16, MQ // 2), BF),
        pltpu.VMEM((BLKS, 8, MQ), F32),
        pltpu.VMEM((24, MODW), BF),
        pltpu.VMEM((L, D), BF),
        pltpu.VMEM((L, D), BF),
        pltpu.VMEM((L, F), BF),
        pltpu.VMEM((L, F), BF),
        pltpu.VMEM((3 * hpd, L, HD), BF),
        pltpu.VMEM((L, hpd + 1), F32),
        pltpu.VMEM((BLKS, T, Q), BF),
        pltpu.VMEM((BLKS, T, Q), BF),
        pltpu.VMEM((BLKS, T, Q), BF),
        pltpu.VMEM((T, D), F32),
        pltpu.VMEM((T, D), F32),
        pltpu.VMEM((T, D), F32),
        pltpu.VMEM((L, D), BF),
        pltpu.VMEM((3, T, D), BF),
        pltpu.VMEM((3, T, D), BF),
        pltpu.VMEM((F, D), BF),
        pltpu.VMEM((D, F), BF),
        pltpu.VMEM((Q, D), BF),
        pltpu.VMEM((2, nz, R, D), BF),
        pltpu.VMEM((2, nz, R, F), BF),
        pltpu.VMEM((2, nz, R, CP), BF),
        pltpu.VMEM((R, D), BF),
        pltpu.VMEM((nz - 1, R, D), BF),
        pltpu.VMEM((R, D), BF),
        pltpu.VMEM((L, HD), F32),
        pltpu.VMEM((L, HD), F32),
        pltpu.VMEM((8, WE), F32),
        pltpu.VMEM((8, WL), F32),
        pltpu.VMEM((BLKS, 16, WE // 8), BF),
        pltpu.VMEM((BLKS, 16, WL // 8), BF),
        pltpu.VMEM((BLKS, 16, WE // 8), BF),
        pltpu.VMEM((BLKS, 16, WL // 8), BF),
        pltpu.VMEM((n, 8, R), F32),
        dma((18,)),
        dma((4, 4, nz)), dma((4, 4, nz)), dma((1,)), dma((1,)),
        dma((n,)), dma((n,)), dma((n,)), dma((n,)),
        dma((4,)), dma((4,)),
        dma((4, 3)), dma((4, 3)),
        dma((2, 4)), dma((2, 4)),
        dma((3, 3)), dma((3, 3)),
        dma((3, 4, nz)), dma((3, 4, nz)),
        dma((3, 3)), dma((3, 3)),
        dma((2, 4)), dma((2, 4)), dma((2, n)), dma((2, n)), dma((2, 4)), dma((2, 4)),
        dma((n,)), dma((n,)),
        dma((nz + 2,)), dma((nz + 2,)),
    ]
    in_specs = [vm] * 10 + [hbm] * 5
    out_specs = [vm] * 6 + [hbm] * 5
    return pl.pallas_call(
        functools.partial(layer_kernel, dims),
        out_shape=out_shape,
        in_specs=in_specs,
        out_specs=out_specs,
        scratch_shapes=scratch,
        compiler_params=pltpu.CompilerParams(
            collective_id=0, has_side_effects=True, vmem_limit_bytes=63 << 20
        ),
        name="layer",
    )(*inputs)


def finish_kernel(dims, *refs):
    T, D, n, sub, R, Q, HD, hpd, F, Fr, MODW = dims
    CP, QP = up_to(3 * Q, 128), up_to(Q, 128)
    WE, WL = up_to(5 * D, 1024), up_to(2 * D + 4 * QP, 1024)
    HE, HL = WE // 8, WL // 8
    (
        cond_in, cond_rx, dcond, ball_e, ball_l, gd, gu, gq, gw, out_h, gtok_h,
        gcond_o, gqb_o, gvb_o, gob_o, gub_o, gdb_o, gab_o, ga_h, gq_h, gw_h, gu_h, gd_h, out_to, gtok_to,
        stage, sem, *staged,
    ) = refs
    sources = (cond_rx, dcond, ball_e, ball_l, gd, gu, gq, gw, out_h, gtok_h)
    loads = [pltpu.make_async_copy(src, to, sem.at[stage.shape[0] + 2 + i]) for i, (src, to) in enumerate(zip(sources, staged))]
    for copy in loads:
        copy.start()
    cond_rx, dcond, ball_e, ball_l, gd, gu, gq, gw, out_h, gtok_h = staged
    crops = cond_in.shape[0]
    moves = [
        pltpu.make_async_copy(out_h, out_to, sem.at[stage.shape[0]]),
        pltpu.make_async_copy(gtok_h, gtok_to, sem.at[stage.shape[0] + 1]),
    ]

    def put(value, dest):
        slot = len(moves) - 2
        stage[slot] = value
        copy = pltpu.make_async_copy(stage.at[slot], dest, sem.at[slot])
        copy.start()
        moves.append(copy)

    def columns(dest, p):
        return dest.at[:, pl.ds(D * p, D)]

    for copy in loads:
        copy.wait()
    for copy in moves:
        copy.start()
    for j in range(BLKS):
        put(gd[j].astype(F32), gd_h.at[pl.ds(Fr * j, Fr), :])
    for p in range(3):
        put(jnp.concatenate([gq[j, :, Q * p : Q * (p + 1)] for j in range(BLKS)], axis=1).astype(F32), columns(gq_h, p))
    put(gw[...].astype(F32), gw_h)
    for p in range(BLKS):
        width = n // BLKS
        own = [gu[j, :, Fr * i : Fr * (i + 1)] for i in range(width * p, width * (p + 1)) for j in range(BLKS)]
        put(jnp.concatenate(own, axis=1).astype(F32), columns(gu_h, p))

    cond_all = cond_rx[...].reshape(n * 8, R).astype(BF)

    def crop_rows(ball, chunk, half):
        part = ball[chunk // 2].astype(F32)
        return part[:, 0:8, :] if chunk % 2 == 0 else part[:, 8:16, :]

    chunks_e = [crop_rows(ball_e, c, HE) for c in range(8)]
    chunks_l = [crop_rows(ball_l, c, HL) for c in range(8)]

    def slices(size, first, width):
        at = first
        while at < first + width:
            chunk = at // size
            end = min(first + width, size * (chunk + 1))
            yield chunk, at - size * chunk, end - size * chunk
            at = end

    def crop_sums(chunks, size, first, width):
        got = [jnp.sum(chunks[c][:, :, lo:hi], axis=0) for c, lo, hi in slices(size, first, width)]
        return jnp.concatenate(got, axis=1)

    def crop_grads(chunks, size, first):
        got = [tn(cond_all, chunks[c][:, :, lo:hi].reshape(n * 8, hi - lo).astype(BF)) for c, lo, hi in slices(size, first, D)]
        return jnp.concatenate(got, axis=1)

    every = []
    for p in range(6):
        chunks, size, first = (chunks_l, HL, D * p) if p < 2 else (chunks_e, HE, D * (p - 2))
        put(crop_grads(chunks, size, first), columns(ga_h, p))
        sums = crop_sums(chunks, size, first, D)
        every.append(jnp.sum(sums[:crops], axis=0, keepdims=True))
    biases = crop_sums(chunks_e, HE, 4 * D, D)
    gab_o[...] = jnp.concatenate(every, axis=1).reshape(-1)
    gob_o[...] = biases[0]
    gdb_o[...] = biases[1]
    up_sums = crop_sums(chunks_e, HE, 0, BLKS * F)[7:8]
    own = [up_sums[:, F * j + Fr * i : F * j + Fr * (i + 1)] for i in range(n) for j in range(BLKS)]
    gub_o[...] = jnp.concatenate(own, axis=1).reshape(-1)
    biases = crop_sums(chunks_l, HL, 2 * D, BLKS * QP)
    for row, dest in ((0, gqb_o), (1, gvb_o)):
        own = [biases[row : row + 1, QP * j : QP * j + Q] for j in range(BLKS)]
        dest[...] = jnp.concatenate(own, axis=1).reshape(-1)
    grad = jnp.concatenate([dcond[i] for i in range(n)], axis=1)[:crops]
    cond = cond_in[...].astype(F32)
    gate = 1.0 / (1.0 + jnp.exp(-cond))
    gcond_o[...] = grad * (gate + cond * gate * (1.0 - gate))
    for copy in moves:
        copy.wait()


def run_finish(dims, inputs):
    T, D, n, sub, R, Q, HD, hpd, F, Fr, MODW = dims
    crops = inputs[0].shape[0]
    vm = pl.BlockSpec(memory_space=pltpu.VMEM)
    hbm = pl.BlockSpec(memory_space=pl.ANY)
    small = [(crops, D)] + [(width,) for width in (D, D, D, BLKS * F, D, MODW)]
    large = [(R, MODW), (R, 3 * D), (R, D), (R, BLKS * F), (BLKS * Fr, D)]
    pieces = 4 + 3 + 1 + 4 + 6
    return pl.pallas_call(
        functools.partial(finish_kernel, dims),
        out_shape=[jax.ShapeDtypeStruct(shape, F32) for shape in small + large]
        + [jax.ShapeDtypeStruct((T, D), BF)] * 2,
        in_specs=[vm] + [hbm] * (len(inputs) - 1),
        out_specs=[vm] * len(small) + [hbm] * (len(large) + 2),
        scratch_shapes=[pltpu.VMEM((pieces, R, D), F32), pltpu.SemaphoreType.DMA((pieces + 12,))]
        + [pltpu.VMEM(a.shape, a.dtype) for a in inputs[1:]],
        compiler_params=pltpu.CompilerParams(vmem_limit_bytes=62 << 20),
        name="finish",
    )(*inputs)


def per_device(sub, tokens, condition, segment_ids, qkv_weight, query_bias, value_bias, output_weight, output_bias,
               up_weight, up_bias, down_weight, down_bias, adaln_weight, adaln_bias, cotangent):
    T, D = tokens.shape[1:]
    blks, size = lax.axis_size("blk"), lax.axis_size("dp")
    assert blks == BLKS and tokens.shape[0] == 1
    n = size // sub
    HD = D // HEADS
    hpd = HEADS // blks
    Q = D // blks
    FF = up_weight.shape[1]
    MODW = adaln_weight.shape[1]
    F = FF // blks
    R, Fr = D // n, F // n
    dp = lax.axis_index("dp")
    assert FF == 4 * D and MODW == 6 * D and n % BLKS == 0

    def members(step):
        return [(i, i - i % sub + (i + step) % sub) for i in range(size)]

    def collect(w):
        if sub == 1:
            return w
        full = jnp.zeros((sub,) + w.shape, w.dtype)
        for step in range(sub):
            moved = lax.ppermute(w, "dp", members(step)) if step else w
            full = lax.dynamic_update_index_in_dim(full, moved, (dp - step) % sub, 0)
        return full.reshape((-1,) + w.shape[1:])

    def settle(grad):
        if sub == 1:
            return grad
        parts = grad.reshape((sub, -1) + grad.shape[1:])
        total = 0.0
        for step in range(sub):
            part = lax.dynamic_index_in_dim(parts, (dp + step) % sub, 0, keepdims=False)
            total = total + (lax.ppermute(part, "dp", members(step)) if step else part)
        return total

    def over_members(vector):
        if sub == 1:
            return vector
        total = vector
        for step in range(1, sub):
            total = total + lax.ppermute(vector, "dp", members(step))
        return total

    inputs = (
        tokens[0], cotangent[0], segment_ids, condition[0], query_bias, value_bias, output_bias, down_bias,
        up_bias, adaln_bias, collect(adaln_weight), collect(qkv_weight),
        collect(output_weight), collect(up_weight), collect(down_weight),
    )
    dims = (T, D, n, sub, R, Q, HD, hpd, F, Fr, MODW)
    out, gtok, cond_rx, dcond, ball_e, ball_l, gd, gu, gq, gw, _ = run_layer(dims, inputs)
    done = run_finish(dims, (condition[0], cond_rx, dcond, ball_e, ball_l, gd, gu, gq, gw, out, gtok))
    gcond, gqb, gvb, gob, gub, gdb, gab, ga, gq, gw, gu, gd, out, gtok = done
    gqb, gvb, gob, gub, gdb, gab = (over_members(v) for v in (gqb, gvb, gob, gub, gdb, gab))
    ga, gq, gw, gu, gd = (settle(v) for v in (ga, gq, gw, gu, gd))
    return out[None], gtok[None], gcond[None], gq, gqb, gvb, gw, gob, gu, gub, gd, gdb, ga, gab


def solution(mesh):
    rows, strips = P("dp", None), P("dp", "blk", None)
    in_specs = (
        strips, P("dp", None, None), rows, rows, P(), P(), rows, P(), rows, P(), rows, P(), rows, P(), strips,
    )
    out_specs = (
        strips, strips, P("dp", None, None), rows, P(), P(), rows, P(), rows, P(), rows, P(), rows, P(),
    )

    def whole(*args):
        size = mesh.shape["dp"]
        rows_each = args[3].shape[0] // size
        sub = 1
        while (rows_each * sub) % 16:
            sub *= 2
        body = functools.partial(per_device, sub)
        return jax.shard_map(body, mesh=mesh, in_specs=in_specs, out_specs=out_specs, check_vma=False)(*args)

    return whole
```

time: 436 us -> 289 us (0.66)
  local copies, waits for them, and re-layouts: 73.1 us -> 1.41 us
  Pallas kernels: 331 us -> 283 us
  starting transfers between devices: 15 us -> 0 us
  other arithmetic: 7.18 us -> 0 us
    pallas_call x1, Pallas kernels: 331 us -> 274 us  [run_layer(): pl.pallas_call(functools.partial(layer_kernel, dims), out_shape=out_shape...]
    reshape x19 -> x0, local copies, waits for them, and re-layouts: 45.2 us -> none  [the longest x3 19.3 us: per_device(): gu.astype(F32).reshape(blks, R, n, Fr).transpose(1, 2, 0, 3).reshape(R, FF)]
    ppermute x7 -> x0, starting transfers between devices: 15 us -> none  [cond_rows_all(): moved = lax.ppermute(part, 'dp', perm) if step else part]
    pallas_call x0 -> x1, Pallas kernels: none -> 9.27 us  [run_finish(): pl.pallas_call(functools.partial(finish_kernel, dims), out_shape=[jax.Sha...]
    dynamic_slice x4 -> x0, local copies, waits for them, and re-layouts: 7.78 us -> none  [the longest x3 6.06 us: pick(): lax.dynamic_index_in_dim(w.reshape(w.shape[0], groups, blks, width), b, 2...]
    unnamed x60 -> x1, local copies, waits for them, and re-layouts: 6.98 us -> 1.41 us
    broadcast_in_dim x11 -> x0, local copies, waits for them, and re-layouts: 5.26 us -> none  [the longest x7 3.43 us: cond_rows_all(): full = lax.dynamic_update_index_in_dim(full, moved, (g - step) % n, 0)]
  transfers between devices with their start and end apart: 7 -> 0, of which waited for: 0 -> 0; matrix products, arithmetic and copies ran while one was open for 17% -> 0% of each run, Pallas kernels for 77% -> 0%
where the time goes in v2:
time: 289 us; the launch traced here: 285 us
  Pallas kernels  283 us (98%)
    pallas_call x1, Pallas kernels, run_layer(): pl.pallas_call(functools.partial(layer_kernel, dims), out_shape=out_shape...  274 us
    pallas_call x1, Pallas kernels, run_finish(): pl.pallas_call(functools.partial(finish_kernel, dims), out_shape=[jax.Sha...  9.27 us

profile of v2, /device:TPU:0, one launch (start us, length us, event | category | flops | bytes accessed | tf_op | source)
XLA Modules:
  0.0 285.1 jit_solution(14943293139383650799)
XLA Ops:
  0.7 273.6 %layer.1 = (bf16[256,1152]{1,0:T(8,128)(2,1)}, bf16[256,1152]{1,0:T(8,128)(2,1)}, f32[8,8,144]{2,1,0:T(8,128)}, f32[8,8,144]{2,1,0:T(8,128)}, bf16[4,8,16,768]{3...) custom-call(bf16[256,1152]{1,0:T(8,128)(2,1)} %bitcast.6, ...), custom_call_target="tpu_custom_call" | custom-call | tf_op jit(solution)/shard_map/layer/pallas_call | solution.py:1009
  274.3 9.3 %finish.1 = (f32[7,1152]{1,0:T(8,128)}, f32[1152]{0:T(1024)}, f32[1152]{0:T(1024)}, f32[1152]{0:T(1024)}, f32[4608]{0:T(1024)}, /*index=5*/f32[1152]{0:T(1024)},...) custom-call(bf16[7,1152]{1,0:T(8,128)(2,1)} %bitcast.9, ...), custom_call_target="tpu_custom_call" | custom-call | tf_op jit(solution)/shard_map/finish/pallas_call | solution.py:1125
  283.5 1.4 copy.29
